TPU v7x, 256 devices: a whole 4x4x8 slice. The times are simulated.
256 devices in a mesh: ns: 16 (over x_lo, y, core), ew: 16 (over x_hi, z).
Axes of the slice: x: 4 (x_hi: 2, x_lo: 2; x = x_hi * 2 + x_lo), y: 4, z: 8, core: 2. Of those that a mesh axis runs over, the one named last changes fastest.
Arguments:
- tokens: bfloat16 [512, 256, 1024], P('ns', 'ew'), may hold values from -6 to 6
- norm_gain: float32 [1024], replicated, may hold values from 0.5 to 1.5
- norm_bias: float32 [1024], replicated, may hold values from -2 to 2
- projection_weight: bfloat16 [1024, 3072], replicated, may hold values from -0.1875 to 0.1875
- projection_bias: float32 [3072], replicated, may hold values from -6 to 6
- context_gain: float32 [1024], replicated, may hold values from 0.5 to 1.5
- context_bias: float32 [1024], replicated, may hold values from -2 to 2
- output_weight: bfloat16 [1024, 1024], replicated, may hold values from -0.1875 to 0.1875
- output_bias: float32 [1024], replicated, may hold values from -2 to 2
- context_positions: int32 [256, 64], replicated, may hold values from 0 to 131071, as said below
Outputs:
- mixed: bfloat16 [512, 256, 1024], P('ns', 'ew')
- context: bfloat16 [256, 1024], replicated
Inputs may be any that keep to these rules, and one draw needn't show every extreme that they name: `context_positions`: the positions of one context token all lie in one square of 16 x 16 grid tokens.
All inputs are finite; a program needn't handle non-finite values.
Results may differ from a plain program's by a relative error of at most 0.0049.
The roundings to bfloat16 on the way count: a program that leaves them out, or rounds other values in their place, can miss the bound.
Values may be sent and summed in bfloat16 or wider, within the bound.
A program may use at most 128 MiB of HBM per device.

v0:
```python
import jax
import jax.numpy as jnp
from jax import lax
from jax.sharding import PartitionSpec as P

HEADS = 16
RADIUS = 7


def with_halo(block, sides, width):
    for axis, dim in sides:
        count = lax.axis_size(axis)
        forward = [(i, i + 1) for i in range(count - 1)]
        backward = [(target, source) for source, target in forward]
        low = lax.ppermute(
            lax.slice_in_dim(block, block.shape[dim] - width, None, axis=dim), axis, forward
        )
        high = lax.ppermute(lax.slice_in_dim(block, 0, width, axis=dim), axis, backward)
        block = jnp.concatenate([low, block, high], axis=dim)
    return block


def layer_norm(inputs, gamma_gain, beta_bias):
    centre = inputs - jnp.mean(inputs, axis=-1, keepdims=True)
    spread = jnp.mean(centre * centre, axis=-1, keepdims=True)
    return centre * lax.rsqrt(spread + 1e-05) * gamma_gain + beta_bias


def neighbour_attention(
    queries, key_rim, value_rim, inside_mask, context_keys, context_values, head_count
):
    tile_rows, tile_cols, features = queries.shape
    head_width = features // head_count
    window_span = key_rim.shape[0] - tile_rows + 1
    rim_cols = key_rim.shape[1]
    score_scale = head_width ** (-0.5)
    band_rows = 8
    band_count = tile_rows // band_rows
    slab_rows = band_rows + window_span - 1
    context_heads_k = context_keys.reshape(-1, head_count, head_width)
    context_heads_v = context_values.reshape(-1, head_count, head_width)
    query_rows = lax.broadcasted_iota(jnp.int32, (band_rows, tile_cols), 0).reshape(-1)
    query_cols = lax.broadcasted_iota(jnp.int32, (band_rows, tile_cols), 1).reshape(-1)
    key_rows = lax.broadcasted_iota(jnp.int32, (slab_rows, rim_cols), 0).reshape(-1)
    key_cols = lax.broadcasted_iota(jnp.int32, (slab_rows, rim_cols), 1).reshape(-1)
    row_gap = key_rows[None, :] - query_rows[:, None]
    col_gap = key_cols[None, :] - query_cols[:, None]
    band_mask = (row_gap >= 0) & (row_gap < window_span) & (col_gap >= 0) & (col_gap < window_span)

    def one_band(band_index):
        start_row = band_index * band_rows
        query_band = lax.dynamic_slice_in_dim(queries, start_row, band_rows, 0).reshape(
            -1, head_count, head_width
        )
        key_slab = lax.dynamic_slice_in_dim(key_rim, start_row, slab_rows, 0).reshape(
            -1, head_count, head_width
        )
        value_slab = lax.dynamic_slice_in_dim(value_rim, start_row, slab_rows, 0).reshape(
            -1, head_count, head_width
        )
        inside_slab = lax.dynamic_slice_in_dim(inside_mask, start_row, slab_rows, 0).reshape(-1)
        keep_mask = band_mask & inside_slab[None, :]
        near_scores = (
            jnp.einsum("qhd,khd->hqk", query_band, key_slab, preferred_element_type=jnp.float32)
            * score_scale
        )
        near_scores = jnp.where(keep_mask[None], near_scores, -1e30)
        context_scores = (
            jnp.einsum(
                "qhd,chd->hqc", query_band, context_heads_k, preferred_element_type=jnp.float32
            )
            * score_scale
        )
        row_maximum = jnp.maximum(jnp.max(near_scores, axis=-1), jnp.max(context_scores, axis=-1))[
            ..., None
        ]
        near_exp = jnp.exp(near_scores - row_maximum)
        context_exp = jnp.exp(context_scores - row_maximum)
        denominator = jnp.sum(near_exp, axis=-1) + jnp.sum(context_exp, axis=-1)
        summed = jnp.einsum(
            "hqk,khd->qhd",
            near_exp.astype(jnp.bfloat16),
            value_slab,
            preferred_element_type=jnp.float32,
        )
        summed = summed + jnp.einsum(
            "hqc,chd->qhd",
            context_exp.astype(jnp.bfloat16),
            context_heads_v,
            preferred_element_type=jnp.float32,
        )
        divisor = jnp.transpose(denominator)[..., None]
        return (summed / divisor).astype(jnp.bfloat16).reshape(band_rows, tile_cols, features)

    banded = lax.map(one_band, jnp.arange(band_count, dtype=jnp.int32))
    return banded.reshape(tile_rows, tile_cols, features)


def on_device(
    tokens,
    norm_gain,
    norm_bias,
    projection_weight,
    projection_bias,
    context_gain,
    context_bias,
    output_weight,
    output_bias,
    context_positions,
):
    tile_rows, tile_cols, features = tokens.shape
    reach_cells = RADIUS
    flat_tokens = tokens.reshape(tile_rows * tile_cols, features)
    normed = layer_norm(flat_tokens.astype(jnp.float32), norm_gain, norm_bias).astype(jnp.bfloat16)
    queries = (
        jnp.dot(normed, projection_weight[:, :features], preferred_element_type=jnp.float32)
        + projection_bias[:features]
    )
    queries = queries.astype(jnp.bfloat16).reshape(tile_rows, tile_cols, features)
    pair_weight = projection_weight[:, features:]
    pair_bias = projection_bias[features:]
    pair_values = (
        jnp.dot(normed, pair_weight, preferred_element_type=jnp.float32) + pair_bias
    ).astype(jnp.bfloat16)
    pair_rim = with_halo(
        pair_values.reshape(tile_rows, tile_cols, 2 * features), (("ns", 0), ("ew", 1)), reach_cells
    )
    total_rows = tile_rows * lax.axis_size("ns")
    total_cols = tile_cols * lax.axis_size("ew")
    first_row = lax.axis_index("ns") * tile_rows
    first_col = lax.axis_index("ew") * tile_cols
    row_ids = first_row - reach_cells + jnp.arange(tile_rows + 2 * reach_cells, dtype=jnp.int32)
    col_ids = first_col - reach_cells + jnp.arange(tile_cols + 2 * reach_cells, dtype=jnp.int32)
    inside_mask = ((row_ids >= 0) & (row_ids < total_rows))[:, None] & (
        (col_ids >= 0) & (col_ids < total_cols)
    )[None, :]
    own_rows = first_row + jnp.arange(tile_rows, dtype=jnp.int32)
    own_cols = first_col + jnp.arange(tile_cols, dtype=jnp.int32)
    own_ids = (own_rows[:, None] * total_cols + own_cols[None, :]).reshape(-1)
    member_counts = jnp.sum(
        (context_positions[:, :, None] == own_ids[None, None, :]).astype(jnp.int32), axis=1
    ).astype(jnp.bfloat16)
    partial_sums = jnp.dot(member_counts, flat_tokens, preferred_element_type=jnp.float32)
    pooled = lax.psum(partial_sums, ("ns", "ew"))
    context = layer_norm(pooled, context_gain, context_bias).astype(jnp.bfloat16)
    context_pairs = (
        jnp.dot(context, pair_weight, preferred_element_type=jnp.float32) + pair_bias
    ).astype(jnp.bfloat16)
    attended = neighbour_attention(
        queries,
        pair_rim[..., :features],
        pair_rim[..., features:],
        inside_mask,
        context_pairs[:, :features],
        context_pairs[:, features:],
        HEADS,
    )
    mixed_out = (
        flat_tokens.astype(jnp.float32)
        + jnp.dot(attended.reshape(-1, features), output_weight, preferred_element_type=jnp.float32)
        + output_bias
    )
    return (mixed_out.astype(jnp.bfloat16).reshape(tile_rows, tile_cols, features), context)


def solution(mesh):
    return jax.shard_map(
        on_device,
        mesh=mesh,
        in_specs=(P("ns", "ew", None), P(), P(), P(), P(), P(), P(), P(), P(), P()),
        out_specs=(P("ns", "ew", None), P()),
        check_vma=False,
    )
```

profile of v0, /device:TPU:2, one launch (start us, length us, event | category | flops | bytes accessed | tf_op | source)
XLA Modules:
  0.0 463.1 jit_solution(16714780746645949682)
XLA Ops:
  12.6 4.9 %add_convert_fusion = bf16[512,2048]{1,0:T(8,128)(2,1)S(1)} fusion(bf16[512,1024]{1,0:T(8,128)(2,1)S(1)} %fusion.49, bf16[1024,3072]{1,0:T(8,128)(2,1)} %param.15, f32[2048]{0:T(1024)S(1)} %slice.43), kind=kOutput, calls=%fused_computation.44 | convolution fusion | flops 2149580800 | bytes 7348224 | tf_op jit(solution)/shard_map/dot_general | solution.py:123
  19.9 4.3 collective-permute-start.1
  27.5 4.9 %convert_reduce_fusion = s32[256,512]{1,0:T(8,128)S(1)} fusion(s32[512]{0:T(512)S(1)} %add.178, s32[256,64]{1,0:T(8,128)S(1)} %copy.48), kind=kLoop, calls=%fused_computation.42 | loop fusion | flops 25034752 | bytes 591872 | tf_op jit(solution)/shard_map/reduce_sum | solution.py:140
  34.0 4.2 add_convert_fusion.1
  38.2 4.1 copy.47
  42.8 4.5 pad_maximum_fusion.3
  48.6 5.6 %collective-permute-start.2 = (bf16[46,7,2048]{2,0,1:T(8,128)(2,1)}, bf16[46,7,2048]{2,0,1:T(8,128)(2,1)}, u32[]{:S(2)}, u32[]{:S(2)}) collective-permute-start(bf16[46,7,2048]{2,0,1:T(8,128)(2,1)} %get-tuple-element.160), channel_id=1, source_target_pairs={{0,1},{1,2},{2,3},{3,4},{4,5},{5,6},{6,7},{7,8},{8,9},{9,10},{10,1... | collective-permute-start | bytes 3956744 | tf_op jit(solution)/shard_map/ppermute | solution.py:15
  54.2 243.0 %all-reduce.2.cloned.1.call-done = f32[256,1024]{1,0:T(8,128)} async-done(((f32[256,1024]{1,0:T(8,128)}), f32[256,1024]{1,0:T(8,128)}) %all-reduce.2.cloned.1.call-update) | async-done | bytes 1048592 | tf_op jit(solution)/shard_map/psum | solution.py:144
  300.4 3.6 fusion.43
  306.2 4.1 pad_maximum_fusion
  311.3 3.2 copy.51
  314.4 3.3 copy.52
  317.7 134.8 %while.11 = (s32[]{:T(128)}, bf16[4,8,16,1024]{3,2,1,0:T(8,128)(2,1)}, s32[4]{0:T(128)S(1)}, bf16[46,30,1024]{2,1,0:T(8,128)(2,1)}, pred[46,30]{1,0:T(8,128)(4,1...) while((s32[]{:T(128)}, ...), condition=%wide.region_11.12_spmd.clone, body=%wide.region_6.11_spmd.clone.sunk | while | flops 500544512 | bytes 72824960 | solution.py:95
  322.6 3.3 constant_dynamic-slice_fusion.9
  325.9 2.8 reshape.172
  328.7 5.8 %fusion.94 = (f32[16,128]{1,0:T(8,128)S(1)}, f32[16,128,660]{1,2,0:T(8,128)}) fusion(pred[128,660]{0,1:T(8,128)(4,1)} %fusion.93, bf16[128,16,64]{0,2,1:T(8,128)(2,1)} %copy.67, bf16[660,16,64]{2,1,0:T(8,128)(2,1)} %reshape.172), kind=kOutput, calls=%fused_computation.3.clone.1 | convolution fusion | flops 177068032 | bytes 7113216 | tf_op jit(solution)/shard_map/while/body/eval_jaxpr/qhd,khd->hqk/dot_general | solution.py:64
  336.3 4.6 reshape.173
  341.0 5.8 %fusion.95 = f32[128,16,64]{0,2,1:T(8,128)S(1)} fusion(f32[16,128,660]{1,2,0:T(8,128)} %get-tuple-element.252, f32[16,128]{1,0:T(8,128)S(1)} %max.9, pred[128,660]{0,1:T(8,128)(4,1)S(1)} %copy-done.3, bf16[660,16,64]{2,1,0:T(8,128)(2,1)} %reshape.173), kind=kOutput, calls=%fused_computation.18.clone.1 | convolution fusion | flops 178421760 | bytes 7375360 | tf_op jit(solution)/shard_map/while/body/eval_jaxpr/hqk,khd->qhd/dot_general | solution.py:80
  356.3 3.3 constant_dynamic-slice_fusion.9
  362.4 5.8 %fusion.94 = (f32[16,128]{1,0:T(8,128)S(1)}, f32[16,128,660]{1,2,0:T(8,128)}) fusion(pred[128,660]{0,1:T(8,128)(4,1)} %fusion.93, bf16[128,16,64]{0,2,1:T(8,128)(2,1)} %copy.67, bf16[660,16,64]{2,1,0:T(8,128)(2,1)} %reshape.172), kind=kOutput, calls=%fused_computation.3.clone.1 | convolution fusion | flops 177068032 | bytes 7113216 | tf_op jit(solution)/shard_map/while/body/eval_jaxpr/qhd,khd->hqk/dot_general | solution.py:64
  370.0 4.6 reshape.173
  374.7 5.8 %fusion.95 = f32[128,16,64]{0,2,1:T(8,128)S(1)} fusion(f32[16,128,660]{1,2,0:T(8,128)} %get-tuple-element.252, f32[16,128]{1,0:T(8,128)S(1)} %max.9, pred[128,660]{0,1:T(8,128)(4,1)S(1)} %copy-done.3, bf16[660,16,64]{2,1,0:T(8,128)(2,1)} %reshape.173), kind=kOutput, calls=%fused_computation.18.clone.1 | convolution fusion | flops 178421760 | bytes 7375360 | tf_op jit(solution)/shard_map/while/body/eval_jaxpr/hqk,khd->qhd/dot_general | solution.py:80
  390.0 3.3 constant_dynamic-slice_fusion.9
  393.3 2.8 reshape.172
  396.1 5.8 %fusion.94 = (f32[16,128]{1,0:T(8,128)S(1)}, f32[16,128,660]{1,2,0:T(8,128)}) fusion(pred[128,660]{0,1:T(8,128)(4,1)} %fusion.93, bf16[128,16,64]{0,2,1:T(8,128)(2,1)} %copy.67, bf16[660,16,64]{2,1,0:T(8,128)(2,1)} %reshape.172), kind=kOutput, calls=%fused_computation.3.clone.1 | convolution fusion | flops 177068032 | bytes 7113216 | tf_op jit(solution)/shard_map/while/body/eval_jaxpr/qhd,khd->hqk/dot_general | solution.py:64
  403.7 4.6 reshape.173
  408.4 5.8 %fusion.95 = f32[128,16,64]{0,2,1:T(8,128)S(1)} fusion(f32[16,128,660]{1,2,0:T(8,128)} %get-tuple-element.252, f32[16,128]{1,0:T(8,128)S(1)} %max.9, pred[128,660]{0,1:T(8,128)(4,1)S(1)} %copy-done.3, bf16[660,16,64]{2,1,0:T(8,128)(2,1)} %reshape.173), kind=kOutput, calls=%fused_computation.18.clone.1 | convolution fusion | flops 178421760 | bytes 7375360 | tf_op jit(solution)/shard_map/while/body/eval_jaxpr/hqk,khd->qhd/dot_general | solution.py:80
  423.7 3.3 constant_dynamic-slice_fusion.9
  429.8 5.8 %fusion.94 = (f32[16,128]{1,0:T(8,128)S(1)}, f32[16,128,660]{1,2,0:T(8,128)}) fusion(pred[128,660]{0,1:T(8,128)(4,1)} %fusion.93, bf16[128,16,64]{0,2,1:T(8,128)(2,1)} %copy.67, bf16[660,16,64]{2,1,0:T(8,128)(2,1)} %reshape.172), kind=kOutput, calls=%fused_computation.3.clone.1 | convolution fusion | flops 177068032 | bytes 7113216 | tf_op jit(solution)/shard_map/while/body/eval_jaxpr/qhd,khd->hqk/dot_general | solution.py:64
  437.4 4.6 reshape.173
  442.1 5.8 %fusion.95 = f32[128,16,64]{0,2,1:T(8,128)S(1)} fusion(f32[16,128,660]{1,2,0:T(8,128)} %get-tuple-element.252, f32[16,128]{1,0:T(8,128)S(1)} %max.9, pred[128,660]{0,1:T(8,128)(4,1)S(1)} %copy-done.3, bf16[660,16,64]{2,1,0:T(8,128)(2,1)} %reshape.173), kind=kOutput, calls=%fused_computation.18.clone.1 | convolution fusion | flops 178421760 | bytes 7375360 | tf_op jit(solution)/shard_map/while/body/eval_jaxpr/hqk,khd->qhd/dot_general | solution.py:80
  452.5 3.8 fusion.51
  (241 shorter events, 68.4 us)
Async XLA Ops:
  7.2 445.3 %copy-start = (bf16[1024,1024]{1,0:T(8,128)(2,1)S(1)}, bf16[1024,1024]{1,0:T(8,128)(2,1)}, u32[]{:S(2)}) copy-start(bf16[1024,1024]{1,0:T(8,128)(2,1)} %param.19) | copy-start | bytes 6291460
  7.2 290.0 %all-reduce.2.cloned.1.call-start = ((), (), s32[]{:S(2)}) async-start(), calls=%async_computation | async-start | bytes 2097152 | tf_op jit(solution)/shard_map/psum | solution.py:144
  12.5 4.9 %copy-start.8 = (bf16[512,1024]{1,0:T(8,128)(2,1)}, bf16[512,1024]{1,0:T(8,128)(2,1)S(1)}, u32[]{:S(2)}) copy-start(bf16[512,1024]{1,0:T(8,128)(2,1)S(1)} %fusion.49) | copy-start | bytes 3145732
  18.8 8.6 %copy-start.11 = (s32[256,64]{0,1:T(8,128)S(1)}, s32[256,64]{0,1:T(8,128)}, u32[]{:S(2)}) copy-start(s32[256,64]{0,1:T(8,128)} %param.21) | copy-start | bytes 196612
  19.9 22.8 %collective-permute-start.1 = (bf16[7,16,2048]{2,0,1:T(8,128)(2,1)}, bf16[7,16,2048]{2,0,1:T(8,128)(2,1)}, u32[]{:S(2)}, u32[]{:S(2)}) collective-permute-start(bf16[7,16,2048]{2,0,1:T(8,128)(2,1)} %copy.46), channel_id=1, source_target_pairs={{16,0},{32,16},{48,32},{64,48},{80,64},{96,80},{112,96},{128,112},... | collective-permute-start | bytes 1376264 | tf_op jit(solution)/shard_map/ppermute | solution.py:18
  24.2 9.7 %slice-start.2 = ((f32[3072]{0:T(1024)}), f32[1024]{0:T(1024)S(1)}, s32[]{:S(2)}) async-start(f32[3072]{0:T(1024)} %param.16), calls=%async_computation.3 | async-start | bytes 8192 | tf_op jit(solution)/shard_map/slice | solution.py:117
  25.3 17.4 %collective-permute-start = (bf16[7,16,2048]{2,0,1:T(8,128)(2,1)}, bf16[7,16,2048]{2,0,1:T(8,128)(2,1)}, u32[]{:S(2)}, u32[]{:S(2)}) collective-permute-start(bf16[7,16,2048]{2,0,1:T(8,128)(2,1)} %copy.45), channel_id=1, source_target_pairs={{0,16},{16,32},{32,48},{48,64},{64,80},{80,96},{96,112},{112,128},... | collective-permute-start | bytes 1376264 | tf_op jit(solution)/shard_map/ppermute | solution.py:15
  42.7 257.4 %copy-start.16 = (f32[1024]{0:T(1024)S(1)}, f32[1024]{0:T(1024)}, u32[]{:S(2)}) copy-start(f32[1024]{0:T(1024)} %param.18) | copy-start | bytes 12292
  42.7 257.4 %copy-start.17 = (f32[1024]{0:T(1024)S(1)}, f32[1024]{0:T(1024)}, u32[]{:S(2)}) copy-start(f32[1024]{0:T(1024)} %param.17) | copy-start | bytes 12292
  47.3 258.9 %collective-permute-start.3 = (bf16[46,7,2048]{2,0,1:T(8,128)(2,1)}, bf16[46,7,2048]{2,0,1:T(8,128)(2,1)}, u32[]{:S(2)}, u32[]{:S(2)}) collective-permute-start(bf16[46,7,2048]{2,0,1:T(8,128)(2,1)} %get-tuple-element.161), channel_id=1, source_target_pairs={{1,0},{2,1},{3,2},{4,3},{5,4},{6,5},{7,6},{8,7},{9,8},{10,9},{11,1... | collective-permute-start | bytes 3956744 | tf_op jit(solution)/shard_map/ppermute | solution.py:18
  48.6 257.6 %collective-permute-start.2 = (bf16[46,7,2048]{2,0,1:T(8,128)(2,1)}, bf16[46,7,2048]{2,0,1:T(8,128)(2,1)}, u32[]{:S(2)}, u32[]{:S(2)}) collective-permute-start(bf16[46,7,2048]{2,0,1:T(8,128)(2,1)} %get-tuple-element.160), channel_id=1, source_target_pairs={{0,1},{1,2},{2,3},{3,4},{4,5},{5,6},{6,7},{7,8},{8,9},{9,10},{10,1... | collective-permute-start | bytes 3956744 | tf_op jit(solution)/shard_map/ppermute | solution.py:15
  328.7 5.8 %copy-start.2 = (bf16[128,16,64]{0,2,1:T(8,128)(2,1)S(1)}, bf16[128,16,64]{0,2,1:T(8,128)(2,1)}, u32[]{:S(2)}) copy-start(bf16[128,16,64]{0,2,1:T(8,128)(2,1)} %copy.67) | copy-start | bytes 786436 | tf_op jit(solution)/shard_map/while
  328.7 5.8 %copy-start.4 = (bf16[256,16,64]{0,2,1:T(8,128)(2,1)S(1)}, bf16[256,16,64]{0,2,1:T(8,128)(2,1)}, u32[]{:S(2)}) copy-start(bf16[256,16,64]{0,2,1:T(8,128)(2,1)} %get-tuple-element.300) | copy-start | bytes 1572868 | tf_op jit(solution)/shard_map/while
  336.3 10.4 %slice-start = ((s8[5439488]{0:T(1024)(128)(4,1)}), s8[1245184]{0:T(1024)(128)(4,1)S(1)}, s32[]{:S(2)}) async-start(s8[5439488]{0:T(1024)(128)(4,1)} %bitcast.49), calls=%async_computation.1 | async-start | bytes 2490368 | tf_op jit(solution)/shard_map/while
  341.0 5.8 %slice-start.1 = ((s8[5439488]{0:T(1024)(128)(4,1)}), s8[4194304]{0:T(1024)(128)(4,1)S(1)}, s32[]{:S(2)}) async-start(s8[5439488]{0:T(1024)(128)(4,1)} %bitcast.49), calls=%async_computation.2 | async-start | bytes 8388608 | tf_op jit(solution)/shard_map/while
  351.4 4.9 %copy-start.12 = (s32[128]{0:T(128)}, s32[128]{0:T(128)S(1)}, u32[]{:S(2)}) copy-start(s32[128]{0:T(128)S(1)} %get-tuple-element.302) | copy-start | bytes 1540 | tf_op jit(solution)/shard_map/while
  351.4 4.9 %copy-start.14 = (s32[128]{0:T(128)}, s32[128]{0:T(128)S(1)}, u32[]{:S(2)}) copy-start(s32[128]{0:T(128)S(1)} %get-tuple-element.304) | copy-start | bytes 1540 | tf_op jit(solution)/shard_map/while
  362.4 5.8 %copy-start.2 = (bf16[128,16,64]{0,2,1:T(8,128)(2,1)S(1)}, bf16[128,16,64]{0,2,1:T(8,128)(2,1)}, u32[]{:S(2)}) copy-start(bf16[128,16,64]{0,2,1:T(8,128)(2,1)} %copy.67) | copy-start | bytes 786436 | tf_op jit(solution)/shard_map/while
  362.4 5.8 %copy-start.4 = (bf16[256,16,64]{0,2,1:T(8,128)(2,1)S(1)}, bf16[256,16,64]{0,2,1:T(8,128)(2,1)}, u32[]{:S(2)}) copy-start(bf16[256,16,64]{0,2,1:T(8,128)(2,1)} %get-tuple-element.300) | copy-start | bytes 1572868 | tf_op jit(solution)/shard_map/while
  370.0 10.4 %slice-start = ((s8[5439488]{0:T(1024)(128)(4,1)}), s8[1245184]{0:T(1024)(128)(4,1)S(1)}, s32[]{:S(2)}) async-start(s8[5439488]{0:T(1024)(128)(4,1)} %bitcast.49), calls=%async_computation.1 | async-start | bytes 2490368 | tf_op jit(solution)/shard_map/while
  374.7 5.8 %slice-start.1 = ((s8[5439488]{0:T(1024)(128)(4,1)}), s8[4194304]{0:T(1024)(128)(4,1)S(1)}, s32[]{:S(2)}) async-start(s8[5439488]{0:T(1024)(128)(4,1)} %bitcast.49), calls=%async_computation.2 | async-start | bytes 8388608 | tf_op jit(solution)/shard_map/while
  385.1 4.9 %copy-start.12 = (s32[128]{0:T(128)}, s32[128]{0:T(128)S(1)}, u32[]{:S(2)}) copy-start(s32[128]{0:T(128)S(1)} %get-tuple-element.302) | copy-start | bytes 1540 | tf_op jit(solution)/shard_map/while
  385.1 4.9 %copy-start.14 = (s32[128]{0:T(128)}, s32[128]{0:T(128)S(1)}, u32[]{:S(2)}) copy-start(s32[128]{0:T(128)S(1)} %get-tuple-element.304) | copy-start | bytes 1540 | tf_op jit(solution)/shard_map/while
  396.1 5.8 %copy-start.2 = (bf16[128,16,64]{0,2,1:T(8,128)(2,1)S(1)}, bf16[128,16,64]{0,2,1:T(8,128)(2,1)}, u32[]{:S(2)}) copy-start(bf16[128,16,64]{0,2,1:T(8,128)(2,1)} %copy.67) | copy-start | bytes 786436 | tf_op jit(solution)/shard_map/while
  396.1 5.8 %copy-start.4 = (bf16[256,16,64]{0,2,1:T(8,128)(2,1)S(1)}, bf16[256,16,64]{0,2,1:T(8,128)(2,1)}, u32[]{:S(2)}) copy-start(bf16[256,16,64]{0,2,1:T(8,128)(2,1)} %get-tuple-element.300) | copy-start | bytes 1572868 | tf_op jit(solution)/shard_map/while
  403.7 10.4 %slice-start = ((s8[5439488]{0:T(1024)(128)(4,1)}), s8[1245184]{0:T(1024)(128)(4,1)S(1)}, s32[]{:S(2)}) async-start(s8[5439488]{0:T(1024)(128)(4,1)} %bitcast.49), calls=%async_computation.1 | async-start | bytes 2490368 | tf_op jit(solution)/shard_map/while
  408.4 5.8 %slice-start.1 = ((s8[5439488]{0:T(1024)(128)(4,1)}), s8[4194304]{0:T(1024)(128)(4,1)S(1)}, s32[]{:S(2)}) async-start(s8[5439488]{0:T(1024)(128)(4,1)} %bitcast.49), calls=%async_computation.2 | async-start | bytes 8388608 | tf_op jit(solution)/shard_map/while
  418.8 4.9 %copy-start.12 = (s32[128]{0:T(128)}, s32[128]{0:T(128)S(1)}, u32[]{:S(2)}) copy-start(s32[128]{0:T(128)S(1)} %get-tuple-element.302) | copy-start | bytes 1540 | tf_op jit(solution)/shard_map/while
  429.8 5.8 %copy-start.2 = (bf16[128,16,64]{0,2,1:T(8,128)(2,1)S(1)}, bf16[128,16,64]{0,2,1:T(8,128)(2,1)}, u32[]{:S(2)}) copy-start(bf16[128,16,64]{0,2,1:T(8,128)(2,1)} %copy.67) | copy-start | bytes 786436 | tf_op jit(solution)/shard_map/while
  429.8 5.8 %copy-start.4 = (bf16[256,16,64]{0,2,1:T(8,128)(2,1)S(1)}, bf16[256,16,64]{0,2,1:T(8,128)(2,1)}, u32[]{:S(2)}) copy-start(bf16[256,16,64]{0,2,1:T(8,128)(2,1)} %get-tuple-element.300) | copy-start | bytes 1572868 | tf_op jit(solution)/shard_map/while
  437.4 10.4 %slice-start = ((s8[5439488]{0:T(1024)(128)(4,1)}), s8[1245184]{0:T(1024)(128)(4,1)S(1)}, s32[]{:S(2)}) async-start(s8[5439488]{0:T(1024)(128)(4,1)} %bitcast.49), calls=%async_computation.1 | async-start | bytes 2490368 | tf_op jit(solution)/shard_map/while
  442.1 5.8 %slice-start.1 = ((s8[5439488]{0:T(1024)(128)(4,1)}), s8[4194304]{0:T(1024)(128)(4,1)S(1)}, s32[]{:S(2)}) async-start(s8[5439488]{0:T(1024)(128)(4,1)} %bitcast.49), calls=%async_computation.2 | async-start | bytes 8388608 | tf_op jit(solution)/shard_map/while
  (35 other events, 106.9 us)
Sparse Core Ops, SparseCore 0:
  34.1 263.0 all-reduce.1
where the time goes:
time: 464 us; the launch traced here: 463 us
  waiting for transfers between devices  243 us (52%)
  local copies, waits for them, and re-layouts  82.5 us (18%)
  matrix products  74.3 us (16%)
  other arithmetic  32.6 us (7%)
  between operations  14.3 us (3%)
  starting transfers between devices  13.2 us (3%)
    psum x1, waiting for transfers between devices, on_device(): pooled = lax.psum(partial_sums, ('ns', 'ew'))  243 us
    dot_general x4, matrix products, one_band(): jnp.einsum('hqk,khd->qhd', near_exp.astype(jnp.bfloat16), value_slab, pre...  23.2 us
    dot_general x4, matrix products, one_band(): jnp.einsum('qhd,khd->hqk', query_band, key_slab, preferred_element_type=j...  23.2 us
    reshape x4, local copies, waits for them, and re-layouts, one_band(): lax.dynamic_slice_in_dim(value_rim, start_row, slab_rows, 0)  18.5 us
    dynamic_slice x4, local copies, waits for them, and re-layouts, one_band(): lax.dynamic_slice_in_dim(key_rim, start_row, slab_rows, 0)  13.1 us
    reshape x4, local copies, waits for them, and re-layouts, one_band(): lax.dynamic_slice_in_dim(key_rim, start_row, slab_rows, 0)  11.4 us
  transfers between devices with their start and end apart: 5, of which 1 were waited for; matrix products, arithmetic and copies ran while one was open for 6% of the time, Pallas kernels for 0%

commit v1 on v0

v1 whole, which is shorter than its diff:
```python
import functools
import jax
import jax.numpy as jnp
from jax import lax
from jax.experimental import pallas as pl
from jax.experimental.pallas import tpu as pltpu
from jax.sharding import PartitionSpec as P

F32 = jnp.float32
BF16 = jnp.bfloat16
NT = (((1,), (1,)), ((), ()))


def norm_rows(x, gain, bias):
    centre = x - jnp.mean(x, axis=-1, keepdims=True)
    spread = jnp.mean(centre * centre, axis=-1, keepdims=True)
    return centre * lax.rsqrt(spread + 1e-05) * gain + bias


def compute(unroll, place_ref, rim, ctx, gain, beta, w, wb, wo, ob, out,
            wq_v, wk_v, wv_v, wo_v, normed, k, v, kc, vc, q2, att, near_bias, s_buf, p_buf, sem):
    copies = [
        pltpu.make_async_copy(w.at[:, pl.ds(1024, 1024)], wk_v, sem.at[0]),
        pltpu.make_async_copy(w.at[:, pl.ds(2048, 1024)], wv_v, sem.at[1]),
        pltpu.make_async_copy(w.at[:, pl.ds(0, 1024)], wq_v, sem.at[2]),
        pltpu.make_async_copy(wo, wo_v, sem.at[3]),
    ]
    for c in copies:
        c.start()
    row0 = place_ref[0] * 32
    col0 = place_ref[1] * 16

    @pl.loop(0, 12)
    def _(t):
        rows = pl.ds(pl.multiple_of(t * 128, 128), 128)
        normed[rows, :] = norm_rows(rim[rows, :].astype(F32), gain[...], beta[...]).astype(BF16)

    def project(src, dst, weight, bias_at, m, tile):
        @pl.loop(0, m // tile)
        def _(t):
            rows = pl.ds(pl.multiple_of(t * tile, tile), tile)
            for n in range(2):
                cols = slice(n * 512, n * 512 + 512)
                y = jnp.dot(src[rows, :], weight[:, cols], preferred_element_type=F32)
                y = y + wb[:, bias_at + n * 512:bias_at + n * 512 + 512]
                dst[rows, cols] = y.astype(BF16)

    copies[0].wait()
    project(normed, k, wk_v, 1024, 1536, 512)
    project(ctx, kc, wk_v, 1024, 256, 256)
    copies[1].wait()
    project(normed, v, wv_v, 2048, 1536, 512)
    project(ctx, vc, wv_v, 2048, 256, 256)
    copies[2].wait()
    low = lax.broadcasted_iota(jnp.int32, (128, 128), 1) < 64

    @pl.loop(0, 4)
    def _(b):
        rows = pl.ds(pl.multiple_of(b * 256 + 256, 256), 128)
        for n in range(2):
            y = jnp.dot(normed[rows, :], wq_v[:, n * 512:n * 512 + 512], preferred_element_type=F32)
            y = (y + wb[:, n * 512:n * 512 + 512]).astype(BF16).astype(F32) * 0.125
            for i in range(4):
                q = y[:, i * 128:i * 128 + 128]
                q2[b, n * 4 + i, 0:128, :] = jnp.where(low, q, 0.0).astype(BF16)
                q2[b, n * 4 + i, 128:256, :] = jnp.where(low, 0.0, q).astype(BF16)

    copies[3].wait()

    @pl.loop(0, 4)
    def _(b):
        for j in range(6):
            qi = lax.broadcasted_iota(jnp.int32, (128, 128), 0)
            ki = lax.broadcasted_iota(jnp.int32, (128, 128), 1)
            qr = 8 + qi // 16
            qc = 8 + qi % 16
            if j % 2 == 0:
                kr = 8 * (j // 2) + ki // 16
                kc_ = 8 + ki % 16
            else:
                kr = 8 * (j // 2) + (ki % 64) // 8
                kc_ = ki % 8 + jnp.where(ki < 64, 0, 24)
            gr = row0 + 8 * b - 8 + kr
            gc = col0 - 8 + kc_
            ok = ((kr - qr <= 7) & (qr - kr <= 7) & (kc_ - qc <= 7) & (qc - kc_ <= 7)
                  & (gr >= 0) & (gr < 512) & (gc >= 0) & (gc < 256))
            near_bias[:, j * 128:j * 128 + 128] = jnp.where(ok, 0.0, -1e30)

        slab = pl.ds(pl.multiple_of(b * 256, 256), 768)
        qrows = pl.ds(pl.multiple_of(b * 128, 128), 128)

        @pl.loop(0, 8 // unroll)
        def _(po):
            for u in range(unroll):
                p = po * unroll + u
                lanes = pl.ds(pl.multiple_of(p * 128, 128), 128)
                s_ref = s_buf.at[u]
                p_ref = p_buf.at[u]
                q = q2[b, p]
                s_ref[:, 0:256] = lax.dot_general(q, kc[:, lanes], NT, preferred_element_type=F32)
                s_ref[:, 256:1024] = lax.dot_general(q, k[slab, lanes], NT, preferred_element_type=F32)
                ls = []
                for r in range(16):
                    rows = slice(r * 16, r * 16 + 16)
                    mrows = slice((r % 8) * 16, (r % 8) * 16 + 16)
                    sc = s_ref[rows, 0:256]
                    sn = s_ref[rows, 256:1024] + near_bias[mrows, :]
                    s = jnp.concatenate([sc, sn], axis=1)
                    m = jnp.max(s, axis=1, keepdims=True)
                    e = jnp.exp(s - m)
                    ls.append(jnp.sum(e, axis=1, keepdims=True))
                    p_ref[rows, :] = e.astype(BF16)
                o = jnp.dot(p_ref[:, 0:256], vc[:, lanes], preferred_element_type=F32)
                o = o + jnp.dot(p_ref[:, 256:1024], v[slab, lanes], preferred_element_type=F32)
                l = jnp.concatenate(ls, axis=0)
                o = o / l
                att[qrows, lanes] = jnp.where(low, o[0:128], o[128:256]).astype(BF16)

    @pl.loop(0, 4)
    def _(b):
        rows = pl.ds(pl.multiple_of(b * 128, 128), 128)
        src = pl.ds(pl.multiple_of(b * 256 + 256, 256), 128)
        for n in range(2):
            cols = slice(n * 512, n * 512 + 512)
            y = jnp.dot(att[rows, :], wo_v[:, cols], preferred_element_type=F32)
            out[rows, cols] = (rim[src, cols].astype(F32) + y + ob[:, cols]).astype(BF16)


def compute_call(place, rim, ctx, gain, beta, w, wb, wo, ob, unroll=2):
    vm = pl.BlockSpec(memory_space=pltpu.VMEM)
    anyspec = pl.BlockSpec(memory_space=pl.ANY)
    return pl.pallas_call(
        functools.partial(compute, unroll),
        out_shape=jax.ShapeDtypeStruct((512, 1024), BF16),
        in_specs=[pl.BlockSpec(memory_space=pltpu.SMEM), vm, vm, vm, vm, anyspec, vm, anyspec, vm],
        out_specs=vm,
        scratch_shapes=[pltpu.VMEM((1024, 1024), BF16)] * 4 + [
            pltpu.VMEM((1536, 1024), BF16), pltpu.VMEM((1536, 1024), BF16), pltpu.VMEM((1536, 1024), BF16),
            pltpu.VMEM((256, 1024), BF16), pltpu.VMEM((256, 1024), BF16),
            pltpu.VMEM((4, 8, 256, 128), BF16), pltpu.VMEM((512, 1024), BF16),
            pltpu.VMEM((128, 768), F32), pltpu.VMEM((unroll, 256, 1024), F32), pltpu.VMEM((unroll, 256, 1024), BF16),
            pltpu.SemaphoreType.DMA((4,)),
        ],
        compiler_params=pltpu.CompilerParams(vmem_limit_bytes=56 * 2**20),
        name="attend",
    )(place, rim, ctx, gain.reshape(1, -1), beta.reshape(1, -1), w, wb.reshape(1, -1), wo, ob.reshape(1, -1))


MESH = pl.DeviceIdType.MESH


def exchange(tokens, pos, cgain, cbias, rim, ctx,
             send_l, send_r, counts, partial, buf0, p1, buf1, p2, buf2, g,
             halo_s, halo_r, s0, r0, s1, r1, s2, r2, s3, r3, s4, r4):
    ns = lax.axis_index("ns")
    ew = lax.axis_index("ew")
    core = lax.rem(ns, 2)
    unit = ns // 2

    barrier = pltpu.get_barrier_semaphore()

    @pl.loop(1, 16)
    def _(d):
        pl.semaphore_signal(barrier, inc=1, device_id=(lax.rem(ns + d, 16), ew), device_id_type=MESH)
        pl.semaphore_signal(barrier, inc=1, device_id=(ns, lax.rem(ew + d, 16)), device_id_type=MESH)

    @pl.loop(0, 4)
    def _(b):
        x = tokens[pl.ds(pl.multiple_of(b * 128, 128), 128), :]
        rim[b + 1, 0:128, :] = x
        x = x.astype(F32).reshape(8, 2, 8, 1024)
        send_l[b] = x[:, 0].reshape(64, 1024).astype(BF16)
        send_r[b] = x[:, 1].reshape(64, 1024).astype(BF16)

    pl.semaphore_wait(barrier, 30)

    up, down, left, right = (ns - 1, ew), (ns + 1, ew), (ns, ew - 1), (ns, ew + 1)

    def halo(i, src, dst, device):
        return pltpu.make_async_remote_copy(src_ref=src, dst_ref=dst, send_sem=halo_s.at[i], recv_sem=halo_r.at[i],
                                            device_id=device, device_id_type=MESH)
    mid = pl.ds(1, 4)
    go_left = halo(0, send_l, rim.at[mid, pl.ds(192, 64)], left)
    go_right = halo(1, send_r, rim.at[mid, pl.ds(128, 64)], right)
    go_up = halo(2, tokens.at[pl.ds(0, 128)], rim.at[5, pl.ds(0, 128)], up)
    go_down = halo(3, tokens.at[pl.ds(384, 128)], rim.at[0, pl.ds(0, 128)], down)
    corner = {}
    for k, at in ((0, 128), (1, 192)):
        corner[k] = (halo(4 + 2 * k, rim.at[1, pl.ds(at, 64)], rim.at[5, pl.ds(at, 64)], up),
                     halo(5 + 2 * k, rim.at[4, pl.ds(at, 64)], rim.at[0, pl.ds(at, 64)], down))
    has_up, has_down, has_left, has_right = ns > 0, ns < 15, ew > 0, ew < 15
    pl.when(has_left)(go_left.start)
    pl.when(has_right)(go_right.start)
    pl.when(has_up)(go_up.start)
    pl.when(has_down)(go_down.start)

    @pl.when(jnp.logical_not(has_up))
    def _():
        rim[0] = jnp.zeros((256, 1024), BF16)

    @pl.when(jnp.logical_not(has_down))
    def _():
        rim[5] = jnp.zeros((256, 1024), BF16)

    for gone, at in ((ew == 0, 128), (ew == 15, 192)):
        @pl.when(gone)
        def _():
            @pl.loop(0, 6)
            def _(t):
                rim[t, at:at + 64, :] = jnp.zeros((64, 1024), BF16)

    def count(t):
        rows = pl.ds(pl.multiple_of(t * 32, 32), 32)
        at = pos[rows, :]
        lr = (at >> 8) - ns * 32
        lc = (at & 255) - ew * 16
        own = (lr >= 0) & (lr < 32) & (lc >= 0) & (lc < 16)
        own_id = jnp.where(own, lr * 16 + lc, -1)
        ids = lax.broadcasted_iota(jnp.int32, (32, 512), 1)
        total = jnp.zeros((32, 512), F32)
        for p in range(64):
            total = total + jnp.where(own_id[:, p:p + 1] == ids, 1.0, 0.0)
        counts[rows, :] = total.astype(BF16)

    pl.loop(0, 8)(count)

    @pl.loop(0, 2)
    def _(t):
        rows = pl.ds(pl.multiple_of(t * 128, 128), 128)
        for n in range(2):
            cols = slice(n * 512, n * 512 + 512)
            partial[rows, cols] = jnp.dot(counts[rows, :], tokens[:, cols], preferred_element_type=F32)

    pair = pltpu.make_async_remote_copy(
        src_ref=partial.at[pl.ds(pl.multiple_of((1 - core) * 128, 128), 128)], dst_ref=buf0, send_sem=s0, recv_sem=r0,
        device_id=(ns + 1 - 2 * core, ew), device_id_type=MESH)
    pair.start()
    pair.wait()

    @pl.loop(0, 8)
    def _(t):
        p1[t] = (partial[pl.ds(pl.multiple_of(core * 128 + t * 16, 16), 16), :]
                 + buf0[pl.ds(pl.multiple_of(t * 16, 16), 16), :])

    def stage1(d):
        to = lax.rem(unit + d, 8)
        return pltpu.make_async_remote_copy(src_ref=p1.at[to], dst_ref=buf1.at[d], send_sem=s1.at[d], recv_sem=r1.at[d],
                                            device_id=(to * 2 + core, ew), device_id_type=MESH)
    pl.loop(1, 8)(lambda d: stage1(d).start())
    pl.loop(1, 8)(lambda d: stage1(d).wait())
    total = p1[unit]
    for d in range(1, 8):
        total = total + buf1[d]
    for i in range(8):
        p2[:, i, :] = total[:, i * 128:i * 128 + 128]

    def stage2(d):
        to = lax.rem(ew + d, 16)
        return pltpu.make_async_remote_copy(src_ref=p2.at[to], dst_ref=buf2.at[d], send_sem=s2.at[d], recv_sem=r2.at[d],
                                            device_id=(ns, to), device_id_type=MESH)
    pl.loop(1, 16)(lambda d: stage2(d).start())
    pl.loop(1, 16)(lambda d: stage2(d).wait())
    total = p2[ew]
    for d in range(1, 16):
        total = total + buf2[d]
    g[ew] = total

    def stage3(d):
        return pltpu.make_async_remote_copy(src_ref=g.at[ew], dst_ref=g.at[ew], send_sem=s3.at[d], recv_sem=r3.at[d],
                                            device_id=(ns, lax.rem(ew + d, 16)), device_id_type=MESH)

    def stage3_in(d):
        at = lax.rem(ew + 16 - d, 16)
        return pltpu.make_async_remote_copy(src_ref=g.at[at], dst_ref=g.at[at], send_sem=s3.at[d], recv_sem=r3.at[d],
                                            device_id=(ns, at), device_id_type=MESH)
    pl.loop(1, 16)(lambda d: stage3(d).start())

    for k, came in ((0, has_left), (1, has_right)):
        @pl.when(came)
        def _():
            (go_right, go_left)[k].wait_recv()
            pl.when(has_up)(corner[k][0].start)
            pl.when(has_down)(corner[k][1].start)

    @pl.loop(1, 16)
    def _(d):
        stage3(d).wait_send()
        stage3_in(d).wait_recv()

    pooled = jnp.concatenate([g[:, i, :] for i in range(8)], axis=1)
    ctx[core, unit] = norm_rows(pooled, cgain[...], cbias[...]).astype(BF16)

    def stage4(d):
        to = lax.rem(ns + d, 16)
        mine = ctx.at[core, unit]
        return pltpu.make_async_remote_copy(src_ref=mine, dst_ref=mine, send_sem=s4.at[d], recv_sem=r4.at[d],
                                            device_id=(to, ew), device_id_type=MESH)

    def stage4_in(d):
        at = lax.rem(ns + 16 - d, 16)
        theirs = ctx.at[lax.rem(at, 2), at // 2]
        return pltpu.make_async_remote_copy(src_ref=theirs, dst_ref=theirs, send_sem=s4.at[d], recv_sem=r4.at[d],
                                            device_id=(at, ew), device_id_type=MESH)
    pl.loop(1, 16)(lambda d: stage4(d).start())

    @pl.loop(1, 16)
    def _(d):
        stage4(d).wait_send()
        stage4_in(d).wait_recv()

    pl.when(has_left)(go_left.wait_send)
    pl.when(has_right)(go_right.wait_send)
    pl.when(has_up)(go_up.wait_send)
    pl.when(has_down)(go_down.wait_send)
    pl.when(has_down)(go_up.wait_recv)
    pl.when(has_up)(go_down.wait_recv)
    for k, came in ((0, has_left), (1, has_right)):
        pl.when(came & has_up)(corner[k][0].wait_send)
        pl.when(came & has_down)(corner[k][1].wait_send)
        pl.when(came & has_down)(corner[k][0].wait_recv)
        pl.when(came & has_up)(corner[k][1].wait_recv)


def exchange_call(tokens, pos, cgain, cbias):
    vm = pl.BlockSpec(memory_space=pltpu.VMEM)
    dma = pltpu.SemaphoreType.DMA
    return pl.pallas_call(
        exchange,
        out_shape=(jax.ShapeDtypeStruct((6, 256, 1024), BF16), jax.ShapeDtypeStruct((2, 8, 16, 1024), BF16)),
        in_specs=[vm] * 4,
        out_specs=(vm, vm),
        scratch_shapes=[
            pltpu.VMEM((4, 64, 1024), BF16), pltpu.VMEM((4, 64, 1024), BF16),
            pltpu.VMEM((256, 512), BF16), pltpu.VMEM((256, 1024), F32),
            pltpu.VMEM((128, 1024), F32), pltpu.VMEM((8, 16, 1024), F32), pltpu.VMEM((8, 16, 1024), F32),
            pltpu.VMEM((16, 8, 128), F32), pltpu.VMEM((16, 8, 128), F32), pltpu.VMEM((16, 8, 128), F32),
            dma((8,)), dma((8,)), dma, dma, dma((8,)), dma((8,)),
            dma((16,)), dma((16,)), dma((16,)), dma((16,)), dma((16,)), dma((16,)),
        ],
        compiler_params=pltpu.CompilerParams(collective_id=0, has_side_effects=True, vmem_limit_bytes=40 * 2**20),
        name="exchange",
    )(tokens, pos, cgain.reshape(1, -1), cbias.reshape(1, -1))


def on_device(tokens, norm_gain, norm_bias, projection_weight, projection_bias, context_gain, context_bias,
              output_weight, output_bias, context_positions):
    flat = tokens.reshape(512, 1024)
    rim, ctx = exchange_call(flat, context_positions, context_gain, context_bias)
    context = ctx.reshape(256, 1024)
    place = jnp.stack([lax.axis_index("ns"), lax.axis_index("ew")]).astype(jnp.int32)
    mixed = compute_call(place, rim.reshape(1536, 1024), context, norm_gain, norm_bias, projection_weight,
                         projection_bias, output_weight, output_bias)
    return mixed.reshape(32, 16, 1024), context


def solution(mesh):
    return jax.shard_map(
        on_device,
        mesh=mesh,
        in_specs=(P("ns", "ew", None), P(), P(), P(), P(), P(), P(), P(), P(), P()),
        out_specs=(P("ns", "ew", None), P()),
        check_vma=False,
    )
```

time: 464 us -> 99.1 us (0.21)
  waiting for transfers between devices: 243 us -> 0 us
  Pallas kernels: 0 us -> 89.3 us
  local copies, waits for them, and re-layouts: 82.5 us -> 6.76 us
  matrix products: 74.3 us -> 0 us
  other arithmetic: 32.6 us -> 0.59 us
  between operations: 14.3 us -> 0.68 us
  starting transfers between devices: 13.2 us -> 0 us
    psum x1 -> x0, waiting for transfers between devices: 243 us -> none  [on_device(): pooled = lax.psum(partial_sums, ('ns', 'ew'))]
    pallas_call x0 -> x2, Pallas kernels: none -> 89.3 us  [the longest x1 50.5 us: exchange_call(): pl.pallas_call(exchange, out_shape=(jax.ShapeDtypeStruct((6, 256, 1024),...]
    dot_general x21 -> x0, matrix products: 74.3 us -> none  [the longest x4 23.2 us: one_band(): jnp.einsum('hqk,khd->qhd', near_exp.astype(jnp.bfloat16), value_slab, pre...]
    reshape x17 -> x0, local copies, waits for them, and re-layouts: 40 us -> none  [the longest x4 18.5 us: one_band(): lax.dynamic_slice_in_dim(value_rim, start_row, slab_rows, 0)]
    dynamic_slice x16 -> x0, local copies, waits for them, and re-layouts: 19.7 us -> none  [the longest x4 13.1 us: one_band(): lax.dynamic_slice_in_dim(key_rim, start_row, slab_rows, 0)]
    reduce_sum x13 -> x0, other arithmetic: 18.4 us -> none  [the longest x8 7.35 us: one_band(): denominator = jnp.sum(near_exp, axis=-1) + jnp.sum(context_exp, axis=-1)]
    ppermute x4 -> x0, starting transfers between devices: 13.2 us -> none  [the longest x2 7.55 us: with_halo(): lax.ppermute(lax.slice_in_dim(block, block.shape[dim] - width, None, axis...]
    slice x10 -> x0, local copies, waits for them, and re-layouts: 5.91 us -> none  [the longest x2 1.12 us: with_halo(): lax.slice_in_dim(block, block.shape[dim] - width, None, axis=dim)]
  transfers between devices with their start and end apart: 5 -> 0, of which waited for: 1 -> 0; matrix products, arithmetic and copies ran while one was open for 6% -> 0% of each run, Pallas kernels for 0% -> 0%
where the time goes in v1:
time: 99.1 us; the launch traced here: 97.3 us
  Pallas kernels  89.3 us (90%)
  local copies, waits for them, and re-layouts  6.76 us (7%)
    pallas_call x1, Pallas kernels, exchange_call(): pl.pallas_call(exchange, out_shape=(jax.ShapeDtypeStruct((6, 256, 1024),...  50.5 us
    pallas_call x1, Pallas kernels, compute_call(): pl.pallas_call(functools.partial(compute, unroll), out_shape=jax.ShapeDty...  38.7 us
    unnamed x14, local copies, waits for them, and re-layouts  6.76 us

profile of v1, /device:TPU:2, one launch (start us, length us, event | category | flops | bytes accessed | tf_op | source)
XLA Modules:
  0.0 97.3 jit_solution(15531509873099118836)
XLA Ops:
  0.6 0.6 pad_add_fusion.place_ref
  1.2 0.9 copy.12.pos
  2.2 0.0 copy-start.3
  2.2 1.2 %copy-done.3 = bf16[32,16,1024]{2,1,0:T(8,128)(2,1)S(1)} copy-done((bf16[32,16,1024]{2,1,0:T(8,128)(2,1)S(1)}, bf16[32,16,1024]{2,1,0:T(8,128)(2,1)}, u32[]{:S(2)}) %copy-start.3) | copy-done | bytes 1048600
  3.4 0.0 copy-start.4
  3.4 0.7 copy-done.4
  4.1 0.0 copy-start.5
  4.1 0.7 copy-done.5
  4.8 50.5 %exchange.1 = (bf16[6,256,1024]{2,1,0:T(8,128)(2,1)S(1)}, bf16[2,8,16,1024]{3,2,1,0:T(8,128)(2,1)S(1)}) custom-call(bf16[512,1024]{1,0:T(8,128)(2,1)S(1)} %bitcast.15, s32[256,64]{1,0:T(8,128)S(1)} %copy.12.pos, f32[1,1024]{1,0:T(1,128)S(1)} %bitcast.16, f32[1,1024]{1,0:T(1,128)S(1)} %bitcast.17), custom_call_target="tpu_custom_call" | custom-call | tf_op jit(solution)/shard_map/exchange/pallas_call | solution.py:327
  55.3 0.0 copy-start
  55.3 1.6 %copy-done = bf16[6,256,1024]{2,1,0:T(8,128)(2,1)} copy-done((bf16[6,256,1024]{2,1,0:T(8,128)(2,1)}, bf16[6,256,1024]{2,1,0:T(8,128)(2,1)S(1)}, u32[]{:S(2)}) %copy-start) | copy-done | bytes 3145752
  57.0 0.0 copy-start.1
  57.0 0.8 copy-done.1
  57.8 0.0 copy-start.2
  57.8 38.7 %attend.1 = bf16[512,1024]{1,0:T(8,128)(2,1)} custom-call(s32[2]{0:T(128)} %pad_add_fusion.place_ref, bf16[1536,1024]{1,0:T(8,128)(2,1)} %bitcast.12, bf16[256,1024]{1,0:T(8,128)(2,1)} %bitcast.13, f32[1,1024]{1,0:T(1,128)} %bitcast.20, f32[1,1024]{1,0:T(1,128)} %bitcast.21, bf16[1024,3072]{1,0:T(8,128)(2,1)} %w.1, f32[1,3072]{1,0:T(1,128)} %bitcast.19, ...), custom_call_target="tpu_custom_call" | custom-call | tf_op jit(solution)/shard_map/attend/pallas_call | solution.py:132
  96.5 0.0 copy-done.2
  96.5 0.8 copy.14
Async XLA Ops:
  2.2 1.2 %copy-start.3 = (bf16[32,16,1024]{2,1,0:T(8,128)(2,1)S(1)}, bf16[32,16,1024]{2,1,0:T(8,128)(2,1)}, u32[]{:S(2)}) copy-start(bf16[32,16,1024]{2,1,0:T(8,128)(2,1)} %param.10) | copy-start | bytes 3145732
  3.4 0.7 copy-start.4
  4.1 0.7 copy-start.5
  55.3 1.7 %copy-start = (bf16[6,256,1024]{2,1,0:T(8,128)(2,1)}, bf16[6,256,1024]{2,1,0:T(8,128)(2,1)S(1)}, u32[]{:S(2)}) copy-start(bf16[6,256,1024]{2,1,0:T(8,128)(2,1)S(1)} %get-tuple-element.4) | copy-start | bytes 9437188
  57.0 0.8 copy-start.1
  57.8 38.8 %copy-start.2 = (bf16[2,8,16,1024]{3,2,1,0:T(8,128)(2,1)S(1)}, bf16[2,8,16,1024]{3,2,1,0:T(8,128)(2,1)}, u32[]{:S(2)}) copy-start(bf16[2,8,16,1024]{3,2,1,0:T(8,128)(2,1)} %copy-done.1) | copy-start | bytes 1572868

commit v2 on v1

v2 whole, which is shorter than its diff:
```python
import jax
import jax.numpy as jnp
from jax import lax
from jax.experimental import pallas as pl
from jax.experimental.pallas import tpu as pltpu
from jax.sharding import PartitionSpec as P

F32 = jnp.float32
BF16 = jnp.bfloat16
MESH = pl.DeviceIdType.MESH
NT = (((1,), (1,)), ((), ()))
TN = (((0,), (0,)), ((), ()))


def rows_at(start, size):
    return pl.ds(pl.multiple_of(start, size), size)


def norm_rows(x, gain, bias):
    centre = x - jnp.mean(x, axis=-1, keepdims=True)
    spread = jnp.mean(centre * centre, axis=-1, keepdims=True)
    return centre * lax.rsqrt(spread + 1e-05) * gain + bias


def layer(tokens_hbm, pos_hbm, w_hbm, wo_hbm, gain, beta, wb, cgain, cbias, ob, out, ctx_out,
          tokens, pos, wq, wk, wv, wo, normed, k, v, q2, att, near_o, near_m, near_l, near_bias,
          s_a, s_b, p_a, p_b, ml_a, ml_b, cs, cp, cml, kc, vc, ctx,
          rim, send_l, send_r, counts, partial, buf0, p1, buf1, p2, buf2, g,
          load, halo_s, halo_r, s0, r0, s1, r1, s2, r2, s3, r3, s4, r4):
    ns = lax.axis_index("ns")
    ew = lax.axis_index("ew")
    core = lax.rem(ns, 2)
    unit = ns // 2

    barrier = pltpu.get_barrier_semaphore()

    @pl.loop(1, 16)
    def _(d):
        pl.semaphore_signal(barrier, inc=1, device_id=(lax.rem(ns + d, 16), ew), device_id_type=MESH)
        pl.semaphore_signal(barrier, inc=1, device_id=(ns, lax.rem(ew + d, 16)), device_id_type=MESH)

    loads = [pltpu.make_async_copy(a, b, load.at[i]) for i, (a, b) in enumerate((
        (tokens_hbm, tokens), (pos_hbm, pos), (w_hbm.at[:, pl.ds(1024, 1024)], wk), (w_hbm.at[:, pl.ds(2048, 1024)], wv),
        (w_hbm.at[:, pl.ds(0, 1024)], wq), (wo_hbm, wo)))]
    for c in loads:
        c.start()
    loads[0].wait()

    @pl.loop(0, 4)
    def _(b):
        x = tokens[rows_at(b * 128, 128), :].astype(F32).reshape(8, 2, 8, 1024)
        send_l[b] = x[:, 0].reshape(64, 1024).astype(BF16)
        send_r[b] = x[:, 1].reshape(64, 1024).astype(BF16)

    up, down, left, right = (ns - 1, ew), (ns + 1, ew), (ns, ew - 1), (ns, ew + 1)

    def halo(i, src, dst, device):
        return pltpu.make_async_remote_copy(src_ref=src, dst_ref=dst, send_sem=halo_s.at[i], recv_sem=halo_r.at[i],
                                            device_id=device, device_id_type=MESH)
    west, east = pl.ds(128, 64), pl.ds(192, 64)
    go_left = [halo(0, send_l.at[0], rim.at[1, east], left), halo(1, send_l.at[3], rim.at[4, east], left),
               halo(2, send_l.at[pl.ds(1, 2)], rim.at[pl.ds(2, 2), east], left)]
    go_right = [halo(3, send_r.at[0], rim.at[1, west], right), halo(4, send_r.at[3], rim.at[4, west], right),
                halo(5, send_r.at[pl.ds(1, 2)], rim.at[pl.ds(2, 2), west], right)]
    go_up = [halo(6, tokens.at[pl.ds(0, 128)], rim.at[5, pl.ds(0, 128)], up)]
    go_down = [halo(7, tokens.at[pl.ds(384, 128)], rim.at[0, pl.ds(0, 128)], down)]
    west_up = halo(8, rim.at[1, west], rim.at[5, west], up)
    west_down = halo(9, rim.at[4, west], rim.at[0, west], down)
    east_up = halo(10, rim.at[1, east], rim.at[5, east], up)
    east_down = halo(11, rim.at[4, east], rim.at[0, east], down)
    has_up, has_down, has_left, has_right = ns > 0, ns < 15, ew > 0, ew < 15

    def when_all(cond, calls):
        @pl.when(cond)
        def _():
            for c in calls:
                c()

    pl.semaphore_wait(barrier, 30)
    for i in range(3):
        pl.when(has_left)(go_left[i].start)
        pl.when(has_right)(go_right[i].start)
    pl.when(has_up)(go_up[0].start)
    pl.when(has_down)(go_down[0].start)

    @pl.when(jnp.logical_not(has_up))
    def _():
        rim[0] = jnp.zeros((256, 1024), BF16)

    @pl.when(jnp.logical_not(has_down))
    def _():
        rim[5] = jnp.zeros((256, 1024), BF16)

    for gone, at in ((ew == 0, 128), (ew == 15, 192)):
        @pl.when(gone)
        def _():
            @pl.loop(0, 6)
            def _(t):
                rim[t, at:at + 64, :] = jnp.zeros((64, 1024), BF16)

    loads[1].wait()

    @pl.loop(0, 8)
    def _(t):
        at = pos[...]
        lr = (at >> 8) - ns * 32
        lc = (at & 255) - ew * 16
        own = (lr >= 0) & (lr < 32) & (lc >= 0) & (lc < 16)
        own_id = jnp.where(own, lr * 16 + lc, -1)
        ids = lax.broadcasted_iota(jnp.int32, (64, 256), 0) + t * 64
        total = jnp.zeros((64, 256), F32)
        for p in range(64):
            total = total + jnp.where(own_id[p:p + 1, :] == ids, 1.0, 0.0)
        counts[rows_at(t * 64, 64), :] = total.astype(BF16)

    @pl.loop(0, 4)
    def _(t):
        cols = rows_at(t * 256, 256)
        partial[:, cols] = lax.dot_general(counts[...], tokens[:, cols], TN, preferred_element_type=F32)

    pair = pltpu.make_async_remote_copy(
        src_ref=partial.at[rows_at((1 - core) * 128, 128)], dst_ref=buf0, send_sem=s0, recv_sem=r0,
        device_id=(ns + 1 - 2 * core, ew), device_id_type=MESH)
    pair.start()

    def project(weight, bias_at, dst, place):
        @pl.loop(0, 4)
        def _(n):
            cols = rows_at(n * 256, 256)
            y = jnp.dot(normed[...], weight[:, cols], preferred_element_type=F32)
            y = (y + wb[:, rows_at(bias_at + n * 256, 256)]).astype(BF16)
            for i in range(4):
                dst[place[i]:place[i] + 128, cols] = y[i * 128:i * 128 + 128]

    @pl.loop(0, 4)
    def _(i):
        rows = rows_at(i * 128, 128)
        normed[rows, :] = norm_rows(tokens[rows, :].astype(F32), gain[...], beta[...]).astype(BF16)

    mid_own = (256, 512, 768, 1024)
    mid_side = (384, 640, 896, 1152)
    loads[2].wait()
    project(wk, 1024, k, mid_own)
    loads[3].wait()
    project(wv, 2048, v, mid_own)

    pair.wait()

    @pl.loop(0, 8)
    def _(t):
        p1[t] = partial[rows_at(core * 128 + t * 16, 16), :] + buf0[rows_at(t * 16, 16), :]

    def stage1(d):
        to = lax.rem(unit + d, 8)
        return pltpu.make_async_remote_copy(src_ref=p1.at[to], dst_ref=buf1.at[d], send_sem=s1.at[d], recv_sem=r1.at[d],
                                            device_id=(to * 2 + core, ew), device_id_type=MESH)
    pl.loop(1, 8)(lambda d: stage1(d).start())

    low = lax.broadcasted_iota(jnp.int32, (128, 128), 1) < 64
    loads[4].wait()

    @pl.loop(0, 4)
    def _(n):
        cols = rows_at(n * 256, 256)
        y = jnp.dot(normed[...], wq[:, cols], preferred_element_type=F32)
        y = (y + wb[:, cols]).astype(BF16).astype(F32) * 0.125
        for b in range(4):
            for i in range(2):
                q = y[b * 128:b * 128 + 128, i * 128:i * 128 + 128]
                q2[n * 2 + i, b * 256:b * 256 + 128, :] = jnp.where(low, q, 0.0).astype(BF16)
                q2[n * 2 + i, b * 256 + 128:b * 256 + 256, :] = jnp.where(low, 0.0, q).astype(BF16)

    for i in range(2):
        pl.when(has_left)(go_right[i].wait_recv)
        pl.when(has_right)(go_left[i].wait_recv)
    when_all(has_left & has_up, [west_up.start])
    when_all(has_left & has_down, [west_down.start])
    when_all(has_right & has_up, [east_up.start])
    when_all(has_right & has_down, [east_down.start])
    pl.when(has_left)(go_right[2].wait_recv)
    pl.when(has_right)(go_left[2].wait_recv)

    @pl.loop(0, 4)
    def _(i):
        normed[rows_at(i * 128, 128), :] = norm_rows(
            rim[i + 1, 128:256, :].astype(F32), gain[...], beta[...]).astype(BF16)

    project(wk, 1024, k, mid_side)

    pl.loop(1, 8)(lambda d: stage1(d).wait())
    total = p1[unit]
    for d in range(1, 8):
        total = total + buf1[d]
    for i in range(8):
        p2[:, i, :] = total[:, i * 128:i * 128 + 128]

    def stage2(d):
        to = lax.rem(ew + d, 16)
        return pltpu.make_async_remote_copy(src_ref=p2.at[to], dst_ref=buf2.at[d], send_sem=s2.at[d], recv_sem=r2.at[d],
                                            device_id=(ns, to), device_id_type=MESH)
    pl.loop(1, 16)(lambda d: stage2(d).start())

    project(wv, 2048, v, mid_side)

    def stage3(d):
        return pltpu.make_async_remote_copy(src_ref=g.at[ew], dst_ref=g.at[ew], send_sem=s3.at[d], recv_sem=r3.at[d],
                                            device_id=(ns, lax.rem(ew + d, 16)), device_id_type=MESH)

    def stage3_in(d):
        at = lax.rem(ew + 16 - d, 16)
        return pltpu.make_async_remote_copy(src_ref=g.at[at], dst_ref=g.at[at], send_sem=s3.at[d], recv_sem=r3.at[d],
                                            device_id=(ns, at), device_id_type=MESH)

    def stage4(d):
        mine = ctx.at[core, unit]
        return pltpu.make_async_remote_copy(src_ref=mine, dst_ref=mine, send_sem=s4.at[d], recv_sem=r4.at[d],
                                            device_id=(lax.rem(ns + d, 16), ew), device_id_type=MESH)

    def stage4_in(d):
        at = lax.rem(ns + 16 - d, 16)
        theirs = ctx.at[lax.rem(at, 2), at // 2]
        return pltpu.make_async_remote_copy(src_ref=theirs, dst_ref=theirs, send_sem=s4.at[d], recv_sem=r4.at[d],
                                            device_id=(at, ew), device_id_type=MESH)

    s_buf, p_buf, ml_buf = (s_a, s_b), (p_a, p_b), (ml_a, ml_b)

    def soft_rows(s, bias, pb, mlb, at, size):
        rows = slice(at, at + size)
        x = s[rows, :]
        if bias is not None:
            x = x + bias[at % 128:at % 128 + size, :]
        m = jnp.max(x, axis=1, keepdims=True)
        e = jnp.exp(x - m)
        l = jnp.sum(e, axis=1, keepdims=True)
        pb[rows, :] = e.astype(BF16)
        mlb[0, rows, :] = jnp.broadcast_to(m, (size, 128))
        mlb[1, rows, :] = jnp.broadcast_to(l, (size, 128))

    def band_step(t):
        b = lax.rem(t + 1, 4)
        for j in range(6):
            qi = lax.broadcasted_iota(jnp.int32, (128, 128), 0)
            ki = lax.broadcasted_iota(jnp.int32, (128, 128), 1)
            qr = 8 + qi // 16
            qc = 8 + qi % 16
            if j % 2 == 0:
                kr = 8 * (j // 2) + ki // 16
                kc_ = 8 + ki % 16
            else:
                kr = 8 * (j // 2) + (ki % 64) // 8
                kc_ = ki % 8 + jnp.where(ki < 64, 0, 24)
            gr = ns * 32 + 8 * b - 8 + kr
            gc = ew * 16 - 8 + kc_
            ok = ((kr - qr <= 7) & (qr - kr <= 7) & (kc_ - qc <= 7) & (qc - kc_ <= 7)
                  & (gr >= 0) & (gr < 512) & (gc >= 0) & (gc < 256))
            near_bias[:, j * 128:j * 128 + 128] = jnp.where(ok, 0.0, -1e30)

        qrows = rows_at(b * 128, 128)

        def keys(part):
            return rows_at(b * 256 + part * 256, 256)

        def scores(p, part):
            lanes = slice(p * 128, p * 128 + 128)
            s_buf[p % 2][:, part * 256:part * 256 + 256] = lax.dot_general(
                q2[p, rows_at(b * 256, 256), :], k[keys(part), lanes], NT, preferred_element_type=F32)

        for part in range(3):
            scores(0, part)
        for u in range(9):
            o = None
            for part in range(3):
                if u + 1 < 8:
                    scores(u + 1, part)
                if u > 0:
                    lanes = slice((u - 1) * 128, u * 128)
                    term = jnp.dot(p_buf[(u - 1) % 2][:, part * 256:part * 256 + 256], v[keys(part), lanes],
                                   preferred_element_type=F32)
                    o = term if o is None else o + term
                if u < 8:
                    for r in ((0, 5), (5, 10), (10, 16))[part:part + 1]:
                        for c in range(*r):
                            soft_rows(s_buf[u % 2], near_bias, p_buf[u % 2], ml_buf[u % 2], c * 16, 16)
            if u > 0:
                mlb = ml_buf[(u - 1) % 2]
                near_o[qrows, lanes] = jnp.where(low, o[0:128], o[128:256])
                near_m[qrows, lanes] = jnp.where(low, mlb[0, 0:128], mlb[0, 128:256])
                near_l[qrows, lanes] = jnp.where(low, mlb[1, 0:128], mlb[1, 128:256])

    @pl.loop(0, 4)
    def _(t):
        @pl.when(t == 2)
        def _():
            pl.when(has_down)(go_up[0].wait_recv)
            pl.when(has_up)(go_down[0].wait_recv)
            when_all(has_left & has_down, [west_up.wait_recv])
            when_all(has_left & has_up, [west_down.wait_recv])
            when_all(has_right & has_down, [east_up.wait_recv])
            when_all(has_right & has_up, [east_down.wait_recv])

            @pl.loop(0, 4)
            def _(i):
                normed[rows_at(i * 128, 128), :] = norm_rows(
                    rim[i // 2 * 5, rows_at(lax.rem(i, 2) * 128, 128), :].astype(F32), gain[...], beta[...]).astype(BF16)
            ends = (0, 128, 1280, 1408)
            project(wk, 1024, k, ends)
            project(wv, 2048, v, ends)

        band_step(t)

        @pl.when(t == 0)
        def _():
            pl.loop(1, 16)(lambda d: stage2(d).wait())
            total = p2[ew]
            for d in range(1, 16):
                total = total + buf2[d]
            g[ew] = total
            pl.loop(1, 16)(lambda d: stage3(d).start())

        @pl.when(t == 1)
        def _():
            @pl.loop(1, 16)
            def _(d):
                stage3(d).wait_send()
                stage3_in(d).wait_recv()

            pooled = jnp.concatenate([g[:, i, :] for i in range(8)], axis=1)
            ctx[core, unit] = norm_rows(pooled, cgain[...], cbias[...]).astype(BF16)
            pl.loop(1, 16)(lambda d: stage4(d).start())

    @pl.loop(1, 16)
    def _(d):
        stage4(d).wait_send()
        stage4_in(d).wait_recv()

    for i in range(2):
        for j in range(8):
            at = i * 128 + j * 16
            normed[at:at + 16, :] = ctx[i, j]
    give = pltpu.make_async_copy(normed.at[pl.ds(0, 256)], ctx_out, load.at[0])
    give.start()

    for weight, bias_at, dst in ((wk, 1024, kc), (wv, 2048, vc)):
        @pl.loop(0, 4)
        def _(n):
            cols = rows_at(n * 256, 256)
            y = jnp.dot(normed[0:256, :], weight[:, cols], preferred_element_type=F32)
            dst[:, cols] = (y + wb[:, rows_at(bias_at + n * 256, 256)]).astype(BF16)

    @pl.loop(0, 8)
    def _(p):
        lanes = rows_at(p * 128, 128)
        for half in range(2):
            cs[half * 512:half * 512 + 512, :] = lax.dot_general(
                q2[p, half * 512:half * 512 + 512, :], kc[:, lanes], NT, preferred_element_type=F32)
        for c in range(32):
            soft_rows(cs, None, cp, cml, c * 32, 32)
        o = jnp.dot(cp[...], vc[:, lanes], preferred_element_type=F32)
        for b in range(4):
            a0, a1 = slice(b * 256, b * 256 + 128), slice(b * 256 + 128, b * 256 + 256)
            rows = slice(b * 128, b * 128 + 128)
            oc = jnp.where(low, o[a0], o[a1])
            mc = jnp.where(low, cml[0, a0, :], cml[0, a1, :])
            lc = jnp.where(low, cml[1, a0, :], cml[1, a1, :])
            mn = near_m[rows, lanes]
            m = jnp.maximum(mn, mc)
            fn, fc = jnp.exp(mn - m), jnp.exp(mc - m)
            both = near_o[rows, lanes] * fn + oc * fc
            att[rows, lanes] = (both / (near_l[rows, lanes] * fn + lc * fc)).astype(BF16)

    loads[5].wait()

    @pl.loop(0, 4)
    def _(n):
        cols = rows_at(n * 256, 256)
        y = jnp.dot(att[...], wo[:, cols], preferred_element_type=F32)
        out[:, cols] = (tokens[:, cols].astype(F32) + y + ob[:, cols]).astype(BF16)

    give.wait()
    when_all(has_left, [c.wait_send for c in go_left])
    when_all(has_right, [c.wait_send for c in go_right])
    when_all(has_up, [go_up[0].wait_send])
    when_all(has_down, [go_down[0].wait_send])
    when_all(has_left & has_up, [west_up.wait_send])
    when_all(has_left & has_down, [west_down.wait_send])
    when_all(has_right & has_up, [east_up.wait_send])
    when_all(has_right & has_down, [east_down.wait_send])


def on_device(tokens, norm_gain, norm_bias, projection_weight, projection_bias, context_gain, context_bias,
              output_weight, output_bias, context_positions):
    vm = pl.BlockSpec(memory_space=pltpu.VMEM)
    hbm = pl.BlockSpec(memory_space=pl.ANY)
    dma = pltpu.SemaphoreType.DMA

    def f32(*shape):
        return pltpu.VMEM(shape, F32)

    def b16(*shape):
        return pltpu.VMEM(shape, BF16)

    mixed, context = pl.pallas_call(
        layer,
        out_shape=(jax.ShapeDtypeStruct((512, 1024), BF16), jax.ShapeDtypeStruct((256, 1024), BF16)),
        in_specs=[hbm] * 4 + [vm] * 6,
        out_specs=(vm, hbm),
        scratch_shapes=[
            b16(512, 1024), pltpu.VMEM((64, 256), jnp.int32), b16(1024, 1024), b16(1024, 1024), b16(1024, 1024),
            b16(1024, 1024), b16(512, 1024), b16(1536, 1024), b16(1536, 1024), b16(8, 1024, 128), b16(512, 1024),
            f32(512, 1024), f32(512, 1024), f32(512, 1024), f32(128, 768),
            f32(256, 768), f32(256, 768), b16(256, 768), b16(256, 768), f32(2, 256, 128), f32(2, 256, 128),
            f32(1024, 256), b16(1024, 256), f32(2, 1024, 128), b16(256, 1024), b16(256, 1024), b16(2, 8, 16, 1024),
            b16(6, 256, 1024), b16(4, 64, 1024), b16(4, 64, 1024),
            b16(512, 256), f32(256, 1024), f32(128, 1024), f32(8, 16, 1024), f32(8, 16, 1024),
            f32(16, 8, 128), f32(16, 8, 128), f32(16, 8, 128),
            dma((6,)), dma((12,)), dma((12,)), dma, dma, dma((8,)), dma((8,)),
            dma((16,)), dma((16,)), dma((16,)), dma((16,)), dma((16,)), dma((16,)),
        ],
        compiler_params=pltpu.CompilerParams(collective_id=0, has_side_effects=True, vmem_limit_bytes=60 * 2**20),
        name="layer",
    )(tokens.reshape(512, 1024), context_positions.T, projection_weight, output_weight,
      norm_gain.reshape(1, -1), norm_bias.reshape(1, -1), projection_bias.reshape(1, -1),
      context_gain.reshape(1, -1), context_bias.reshape(1, -1), output_bias.reshape(1, -1))
    return mixed.reshape(32, 16, 1024), context


def solution(mesh):
    return jax.shard_map(
        on_device,
        mesh=mesh,
        in_specs=(P("ns", "ew", None), P(), P(), P(), P(), P(), P(), P(), P(), P()),
        out_specs=(P("ns", "ew", None), P()),
        check_vma=False,
    )
```

time: 99.1 us -> 71.6 us (0.72)
  Pallas kernels: 89.3 us -> 65.6 us
  local copies, waits for them, and re-layouts: 6.76 us -> 4.17 us
    pallas_call x2 -> x1, Pallas kernels: 89.3 us -> 65.6 us  [on_device(): pl.pallas_call(layer, out_shape=(jax.ShapeDtypeStruct((512, 1024), BF16),...]
    unnamed x14 -> x2, local copies, waits for them, and re-layouts: 6.76 us -> 4.17 us
where the time goes in v2:
time: 71.6 us; the launch traced here: 70.4 us
  Pallas kernels  65.6 us (92%)
  local copies, waits for them, and re-layouts  4.17 us (6%)
    pallas_call x1, Pallas kernels, on_device(): pl.pallas_call(layer, out_shape=(jax.ShapeDtypeStruct((512, 1024), BF16),...  65.6 us
    unnamed x2, local copies, waits for them, and re-layouts  4.17 us

profile of v2, /device:TPU:2, one launch (start us, length us, event | category | flops | bytes accessed | tf_op | source)
XLA Modules:
  0.0 70.4 jit_solution(3236810836142684885)
XLA Ops:
  0.6 65.6 %layer.1 = (bf16[512,1024]{1,0:T(8,128)(2,1)}, bf16[256,1024]{1,0:T(8,128)(2,1)}) custom-call(bf16[512,1024]{1,0:T(8,128)(2,1)} %bitcast.9, s32[64,256]{1,0:T(8,128)} %bitcast.11, bf16[1024,3072]{1,0:T(8,128)(2,1)} %w_hbm.1, bf16[1024,1024]{1,0:T(8,128)(2,1)} %wo_hbm.1, f32[1,1024]{1,0:T(1,128)} %bitcast.13, f32[1,1024]{1,0:T(1,128)} %bitcast.14, ...), custom_call_target="tpu_custom_call" | custom-call | tf_op jit(solution)/shard_map/layer/pallas_call | solution.py:402
  66.3 2.3 %copy.14 = bf16[32,16,1024]{2,1,0:T(8,128)(2,1)} copy(bf16[32,16,1024]{2,1,0:T(8,128)(2,1)} %bitcast.10) | data formatting | bytes 2097152
  68.6 1.9 %copy.15 = bf16[256,1024]{1,0:T(8,128)(2,1)} copy(bf16[256,1024]{1,0:T(8,128)(2,1)} %get-tuple-element.9) | data formatting | bytes 1048576

commit v3 on v2

v3 whole, which is shorter than its diff:
```python
import jax
import jax.numpy as jnp
from jax import lax
from jax.experimental import pallas as pl
from jax.experimental.pallas import tpu as pltpu
from jax.sharding import PartitionSpec as P

F32 = jnp.float32
BF16 = jnp.bfloat16
MESH = pl.DeviceIdType.MESH
NT = (((1,), (1,)), ((), ()))
TN = (((0,), (0,)), ((), ()))


def rows_at(start, size):
    return pl.ds(pl.multiple_of(start, size), size)


def norm_rows(x, gain, bias):
    centre = x - jnp.mean(x, axis=-1, keepdims=True)
    spread = jnp.mean(centre * centre, axis=-1, keepdims=True)
    return centre * lax.rsqrt(spread + 1e-05) * gain + bias


def layer(tokens_hbm, pos_hbm, w_hbm, wo_hbm, gain_hbm, beta_hbm, wb_hbm, cgain_hbm, cbias_hbm, ob_hbm, out, ctx_out,
          gain, beta, wb, cgain, cbias, ob, pos, field, wall, normed, kvq, att, near_o, near_m, near_l, near_bias,
          s_a, s_b, p_a, p_b, ml_a, ml_b, cs, cp, cml, kvc, ctx,
          rim, send_l, send_r, counts, partial, buf0, p1, buf1, p2, buf2, g,
          load, halo_s, halo_r, s0, r0, s1, r1, s2, r2, s3, r3, s4, r4):
    ns = lax.axis_index("ns")
    ew = lax.axis_index("ew")
    core = lax.rem(ns, 2)
    unit = ns // 2

    barrier = pltpu.get_barrier_semaphore()

    @pl.loop(1, 16)
    def _(d):
        pl.semaphore_signal(barrier, inc=1, device_id=(lax.rem(ns + d, 16), ew), device_id_type=MESH)
        pl.semaphore_signal(barrier, inc=1, device_id=(ns, lax.rem(ew + d, 16)), device_id_type=MESH)

    moves = [(tokens_hbm.at[pl.ds(b * 128, 128)], rim.at[b + 1, pl.ds(0, 128)]) for b in range(4)]
    moves += [(pos_hbm, pos), (gain_hbm, gain), (beta_hbm, beta), (wb_hbm, wb), (cgain_hbm, cgain), (cbias_hbm, cbias),
              (ob_hbm, ob)]
    for t in range(6):
        moves.append((w_hbm.at[:, pl.ds((t * 512 + 1024) % 3072, 512)], wall.at[t]))
    for t in range(2):
        moves.append((wo_hbm.at[:, pl.ds(t * 512, 512)], wall.at[6 + t]))
    loads = [pltpu.make_async_copy(a, b, load.at[i]) for i, (a, b) in enumerate(moves)]
    for c in loads:
        c.start()
    for c in loads[:4]:
        c.wait()

    @pl.loop(0, 4)
    def _(b):
        x = rim[b + 1, 0:128, :].astype(F32).reshape(8, 2, 8, 1024)
        send_l[b] = x[:, 0].reshape(64, 1024).astype(BF16)
        send_r[b] = x[:, 1].reshape(64, 1024).astype(BF16)

    up, down, left, right = (ns - 1, ew), (ns + 1, ew), (ns, ew - 1), (ns, ew + 1)

    def halo(i, src, dst, device):
        return pltpu.make_async_remote_copy(src_ref=src, dst_ref=dst, send_sem=halo_s.at[i], recv_sem=halo_r.at[i],
                                            device_id=device, device_id_type=MESH)
    west, east = pl.ds(128, 64), pl.ds(192, 64)
    go_left = [halo(0, send_l.at[0], rim.at[1, east], left), halo(1, send_l.at[3], rim.at[4, east], left),
               halo(2, send_l.at[pl.ds(1, 2)], rim.at[pl.ds(2, 2), east], left)]
    go_right = [halo(3, send_r.at[0], rim.at[1, west], right), halo(4, send_r.at[3], rim.at[4, west], right),
                halo(5, send_r.at[pl.ds(1, 2)], rim.at[pl.ds(2, 2), west], right)]
    go_up = [halo(6, rim.at[1, pl.ds(0, 128)], rim.at[5, pl.ds(0, 128)], up)]
    go_down = [halo(7, rim.at[4, pl.ds(0, 128)], rim.at[0, pl.ds(0, 128)], down)]
    west_up = halo(8, rim.at[1, west], rim.at[5, west], up)
    west_down = halo(9, rim.at[4, west], rim.at[0, west], down)
    east_up = halo(10, rim.at[1, east], rim.at[5, east], up)
    east_down = halo(11, rim.at[4, east], rim.at[0, east], down)
    has_up, has_down, has_left, has_right = ns > 0, ns < 15, ew > 0, ew < 15

    def when_all(cond, calls):
        @pl.when(cond)
        def _():
            for c in calls:
                c()

    loads[4].wait()
    lr = (pos[...] >> 8) - ns * 32
    lc = (pos[...] & 255) - ew * 16
    own = (lr >= 0) & (lr < 32) & (lc >= 0) & (lc < 16)
    pos[...] = jnp.where(own, (lr & 7) * 16 + lc, -1)
    field[...] = jnp.where(own, lax.shift_left(jnp.ones_like(lr), (lr >> 3) * 8), 0)

    @pl.loop(0, 2)
    def _(t):
        ids = lax.broadcasted_iota(jnp.int32, (64, 256), 0) + t * 64
        total = jnp.zeros((64, 256), jnp.int32)
        for p in range(64):
            total = total + jnp.where(pos[p:p + 1, :] == ids, field[p:p + 1, :], 0)
        for i in range(4):
            part = (total >> (8 * i)) & 255
            counts[rows_at(i * 128 + t * 64, 64), :] = part.astype(F32).astype(BF16)

    pl.semaphore_wait(barrier, 30)
    for i in range(3):
        pl.when(has_left)(go_left[i].start)
        pl.when(has_right)(go_right[i].start)
    pl.when(has_up)(go_up[0].start)
    pl.when(has_down)(go_down[0].start)

    @pl.when(jnp.logical_not(has_up))
    def _():
        rim[0] = jnp.zeros((256, 1024), BF16)

    @pl.when(jnp.logical_not(has_down))
    def _():
        rim[5] = jnp.zeros((256, 1024), BF16)

    for gone, at in ((ew == 0, 128), (ew == 15, 192)):
        @pl.when(gone)
        def _():
            @pl.loop(0, 6)
            def _(t):
                rim[t, at:at + 64, :] = jnp.zeros((64, 1024), BF16)

    own_tokens = rim[1:5, 0:128, :].reshape(512, 1024)
    for t in range(2):
        cols = slice(t * 512, t * 512 + 512)
        partial[:, cols] = lax.dot_general(counts[...], own_tokens[:, cols], TN, preferred_element_type=F32)

    pair = pltpu.make_async_remote_copy(
        src_ref=partial.at[rows_at((1 - core) * 128, 128)], dst_ref=buf0, send_sem=s0, recv_sem=r0,
        device_id=(ns + 1 - 2 * core, ew), device_id_type=MESH)
    pair.start()

    def stage1(d):
        to = lax.rem(unit + d, 8)
        return pltpu.make_async_remote_copy(src_ref=p1.at[to], dst_ref=buf1.at[d], send_sem=s1.at[d], recv_sem=r1.at[d],
                                            device_id=(to * 2 + core, ew), device_id_type=MESH)
    def stage2(d):
        to = lax.rem(ew + d, 16)
        return pltpu.make_async_remote_copy(src_ref=p2.at[to], dst_ref=buf2.at[d], send_sem=s2.at[d], recv_sem=r2.at[d],
                                            device_id=(ns, to), device_id_type=MESH)
    def stage3(d):
        return pltpu.make_async_remote_copy(src_ref=g.at[ew], dst_ref=g.at[ew], send_sem=s3.at[d], recv_sem=r3.at[d],
                                            device_id=(ns, lax.rem(ew + d, 16)), device_id_type=MESH)

    def stage3_in(d):
        at = lax.rem(ew + 16 - d, 16)
        return pltpu.make_async_remote_copy(src_ref=g.at[at], dst_ref=g.at[at], send_sem=s3.at[d], recv_sem=r3.at[d],
                                            device_id=(ns, at), device_id_type=MESH)

    def stage4(d):
        mine = ctx.at[core, unit]
        return pltpu.make_async_remote_copy(src_ref=mine, dst_ref=mine, send_sem=s4.at[d], recv_sem=r4.at[d],
                                            device_id=(lax.rem(ns + d, 16), ew), device_id_type=MESH)

    def stage4_in(d):
        at = lax.rem(ns + 16 - d, 16)
        theirs = ctx.at[lax.rem(at, 2), at // 2]
        return pltpu.make_async_remote_copy(src_ref=theirs, dst_ref=theirs, send_sem=s4.at[d], recv_sem=r4.at[d],
                                            device_id=(at, ew), device_id_type=MESH)

    def start_stage1():
        pair.wait()

        @pl.loop(0, 8)
        def _(t):
            p1[t] = partial[rows_at(core * 128 + t * 16, 16), :] + buf0[rows_at(t * 16, 16), :]
        pl.loop(1, 8)(lambda d: stage1(d).start())

    def start_stage2():
        pl.loop(1, 8)(lambda d: stage1(d).wait())
        total = p1[unit]
        for d in range(1, 8):
            total = total + buf1[d]
        for i in range(8):
            p2[:, i, :] = total[:, i * 128:i * 128 + 128]
        pl.loop(1, 16)(lambda d: stage2(d).start())

    def start_stage3():
        pl.loop(1, 16)(lambda d: stage2(d).wait())
        total = p2[ew]
        for d in range(1, 16):
            total = total + buf2[d]
        g[ew] = total
        pl.loop(1, 16)(lambda d: stage3(d).start())

    def start_stage4():
        @pl.loop(1, 16)
        def _(d):
            stage3(d).wait_send()
            stage3_in(d).wait_recv()

        pooled = jnp.concatenate([g[:, i, :] for i in range(8)], axis=1)
        ctx[core, unit] = norm_rows(pooled, cgain[...], cbias[...]).astype(BF16)
        pl.loop(1, 16)(lambda d: stage4(d).start())

    low = lax.broadcasted_iota(jnp.int32, (128, 128), 1) < 64
    first = jnp.where(low, 0.125, 0.0).astype(BF16)
    second = jnp.where(low, 0.0, 0.125).astype(BF16)

    s_buf, p_buf, ml_buf = (s_a, s_b), (p_a, p_b), (ml_a, ml_b)

    def soft_rows(s, bias, pb, mlb, at, size):
        rows = slice(at, at + size)
        x = s[rows, :]
        if bias is not None:
            x = x + bias[at % 128:at % 128 + size, :]
        m = jnp.max(x, axis=1, keepdims=True)
        e = jnp.exp(x - m)
        l = jnp.sum(e, axis=1, keepdims=True)
        pb[rows, :] = e.astype(BF16)
        mlb[0, rows, :] = jnp.broadcast_to(m, (size, 128))
        mlb[1, rows, :] = jnp.broadcast_to(l, (size, 128))

    def band_step(b):
        for j in range(6):
            qi = lax.broadcasted_iota(jnp.int32, (128, 128), 0)
            ki = lax.broadcasted_iota(jnp.int32, (128, 128), 1)
            qr = 8 + qi // 16
            qc = 8 + qi % 16
            if j % 2 == 0:
                kr = 8 * (j // 2) + ki // 16
                kc_ = 8 + ki % 16
            else:
                kr = 8 * (j // 2) + (ki % 64) // 8
                kc_ = ki % 8 + jnp.where(ki < 64, 0, 24)
            gr = ns * 32 + 8 * b - 8 + kr
            gc = ew * 16 - 8 + kc_
            ok = ((kr - qr <= 7) & (qr - kr <= 7) & (kc_ - qc <= 7) & (qc - kc_ <= 7)
                  & (gr >= 0) & (gr < 512) & (gc >= 0) & (gc < 256))
            near_bias[:, j * 128:j * 128 + 128] = jnp.where(ok, 0.0, -1e30)

        qrows = rows_at(b * 128, 128)

        def keys(part):
            return rows_at(b * 256 + part * 256, 256)

        def scores(p, part):
            lanes = slice(p % 4 * 128, p % 4 * 128 + 128)
            q = kvq[4 + p // 4, rows_at(b * 256 + 256, 128), lanes]
            q = jnp.concatenate([q * first, q * second], axis=0)
            s_buf[p % 2][:, part * 256:part * 256 + 256] = lax.dot_general(
                q, kvq[p // 4, keys(part), lanes], NT, preferred_element_type=F32)

        for part in range(3):
            scores(0, part)
        for u in range(9):
            o = None
            for part in range(3):
                if u + 1 < 8:
                    scores(u + 1, part)
                if u > 0:
                    lanes = slice((u - 1) * 128, u * 128)
                    term = jnp.dot(p_buf[(u - 1) % 2][:, part * 256:part * 256 + 256], kvq[2 + (u - 1) // 4, keys(part), (u - 1) % 4 * 128:(u - 1) % 4 * 128 + 128],
                                   preferred_element_type=F32)
                    o = term if o is None else o + term
                if u < 8:
                    for r in ((0, 5), (5, 10), (10, 16))[part:part + 1]:
                        for c in range(*r):
                            soft_rows(s_buf[u % 2], near_bias, p_buf[u % 2], ml_buf[u % 2], c * 16, 16)
            if u > 0:
                mlb = ml_buf[(u - 1) % 2]
                near_o[qrows, lanes] = jnp.where(low, o[0:128], o[128:256])
                near_m[qrows, lanes] = jnp.where(low, mlb[0, 0:128], mlb[0, 128:256])
                near_l[qrows, lanes] = jnp.where(low, mlb[1, 0:128], mlb[1, 128:256])

    for c in loads[5:17]:
        c.wait()

    @pl.loop(0, 3)
    def _(phase):
        @pl.when(phase == 1)
        def _():
            for i in range(2):
                pl.when(has_left)(go_right[i].wait_recv)
                pl.when(has_right)(go_left[i].wait_recv)
            when_all(has_left & has_up, [west_up.start])
            when_all(has_left & has_down, [west_down.start])
            when_all(has_right & has_up, [east_up.start])
            when_all(has_right & has_down, [east_down.start])
            pl.when(has_left)(go_right[2].wait_recv)
            pl.when(has_right)(go_left[2].wait_recv)

        @pl.when(phase == 2)
        def _():
            start_stage4()
            pl.when(has_down)(go_up[0].wait_recv)
            pl.when(has_up)(go_down[0].wait_recv)
            when_all(has_left & has_down, [west_up.wait_recv])
            when_all(has_left & has_up, [west_down.wait_recv])
            when_all(has_right & has_down, [east_up.wait_recv])
            when_all(has_right & has_up, [east_down.wait_recv])

        ends = phase // 2
        blocks = [(1 - ends) * (2 * i + 2 + phase) + ends * (i // 2 * 10 + i % 2) for i in range(4)]
        groups = [(1 - ends) * (i + 1) + ends * (i // 2 * 5) for i in range(4)]
        sides = [(1 - ends) * phase + ends * (i % 2) for i in range(4)]
        for i in range(4):
            x = rim[groups[i], rows_at(sides[i] * 128, 128), :].astype(F32)
            normed[i * 128:i * 128 + 128, :] = norm_rows(x, gain[...], beta[...]).astype(BF16)

        @pl.loop(0, 4 + 2 * ((2 - phase) // 2))
        def _(t):
            pl.when((phase == 0) & (t == 2))(start_stage1)
            pl.when((phase == 1) & (t == 2))(start_stage2)
            y = jnp.dot(normed[...], wall[t], preferred_element_type=F32)
            y = (y + wb[:, rows_at(lax.rem(t * 512 + 1024, 3072), 512)]).astype(BF16)
            for i in range(4):
                kvq[t, rows_at(blocks[i] * 128, 128), :] = y[i * 128:i * 128 + 128]

        @pl.loop(0, 2 * ((phase + 1) // 2))
        def _(i):
            pl.when((phase == 1) & (i == 0))(start_stage3)
            band_step(lax.rem(2 * phase - 1 + i, 4))

    @pl.loop(1, 16)
    def _(d):
        stage4(d).wait_send()
        stage4_in(d).wait_recv()

    for i in range(2):
        for j in range(8):
            at = i * 128 + j * 16
            normed[at:at + 16, :] = ctx[i, j]
    ctx_out[...] = normed[0:256, :]

    @pl.loop(0, 4)
    def _(t):
        y = jnp.dot(normed[0:256, :], wall[t], preferred_element_type=F32)
        kvc[t] = (y + wb[:, rows_at(t * 512 + 1024, 512)]).astype(BF16)

    @pl.loop(0, 8)
    def _(p):
        lanes = rows_at(p * 128, 128)
        part = rows_at(lax.rem(p, 4) * 128, 128)
        qs = []
        for b in range(4):
            q = kvq[4 + p // 4, b * 256 + 256:b * 256 + 384, part]
            qs += [q * first, q * second]
        cs[...] = lax.dot_general(jnp.concatenate(qs, axis=0), kvc[p // 4, :, part], NT, preferred_element_type=F32)
        for c in range(32):
            soft_rows(cs, None, cp, cml, c * 32, 32)
        o = jnp.dot(cp[...], kvc[2 + p // 4, :, part], preferred_element_type=F32)
        for b in range(4):
            a0, a1 = slice(b * 256, b * 256 + 128), slice(b * 256 + 128, b * 256 + 256)
            rows = slice(b * 128, b * 128 + 128)
            oc = jnp.where(low, o[a0], o[a1])
            mc = jnp.where(low, cml[0, a0, :], cml[0, a1, :])
            lc = jnp.where(low, cml[1, a0, :], cml[1, a1, :])
            mn = near_m[rows, lanes]
            m = jnp.maximum(mn, mc)
            fn, fc = jnp.exp(mn - m), jnp.exp(mc - m)
            both = near_o[rows, lanes] * fn + oc * fc
            att[rows, lanes] = (both / (near_l[rows, lanes] * fn + lc * fc)).astype(BF16)

    for c in loads[17:]:
        c.wait()
    for n in range(2):
        cols = slice(n * 512, n * 512 + 512)
        y = jnp.dot(att[...], wall[6 + n], preferred_element_type=F32)
        for b in range(4):
            rows = slice(b * 128, b * 128 + 128)
            out[rows, cols] = (rim[b + 1, 0:128, cols].astype(F32) + y[rows] + ob[:, cols]).astype(BF16)

    when_all(has_left, [c.wait_send for c in go_left])
    when_all(has_right, [c.wait_send for c in go_right])
    when_all(has_up, [go_up[0].wait_send])
    when_all(has_down, [go_down[0].wait_send])
    when_all(has_left & has_up, [west_up.wait_send])
    when_all(has_left & has_down, [west_down.wait_send])
    when_all(has_right & has_up, [east_up.wait_send])
    when_all(has_right & has_down, [east_down.wait_send])


def on_device(tokens, norm_gain, norm_bias, projection_weight, projection_bias, context_gain, context_bias,
              output_weight, output_bias, context_positions):
    vm = pl.BlockSpec(memory_space=pltpu.VMEM)
    hbm = pl.BlockSpec(memory_space=pltpu.MemorySpace.HBM)
    dma = pltpu.SemaphoreType.DMA

    def f32(*shape):
        return pltpu.VMEM(shape, F32)

    def b16(*shape):
        return pltpu.VMEM(shape, BF16)

    mixed, context = pl.pallas_call(
        layer,
        out_shape=(jax.ShapeDtypeStruct((512, 1024), BF16), jax.ShapeDtypeStruct((256, 1024), BF16)),
        in_specs=[hbm] * 10,
        out_specs=(vm, vm),
        scratch_shapes=[
            f32(1, 1024), f32(1, 1024), f32(1, 3072), f32(1, 1024), f32(1, 1024), f32(1, 1024),
            pltpu.VMEM((64, 256), jnp.int32), pltpu.VMEM((64, 256), jnp.int32), b16(8, 1024, 512), b16(512, 1024),
            b16(6, 1536, 512), b16(512, 1024),
            f32(512, 1024), f32(512, 1024), f32(512, 1024), f32(128, 768),
            f32(256, 768), f32(256, 768), b16(256, 768), b16(256, 768), f32(2, 256, 128), f32(2, 256, 128),
            f32(1024, 256), b16(1024, 256), f32(2, 1024, 128), b16(4, 256, 512), b16(2, 8, 16, 1024),
            b16(6, 256, 1024), b16(4, 64, 1024), b16(4, 64, 1024),
            b16(512, 256), f32(256, 1024), f32(128, 1024), f32(8, 16, 1024), f32(8, 16, 1024),
            f32(16, 8, 128), f32(16, 8, 128), f32(16, 8, 128),
            dma((19,)), dma((12,)), dma((12,)), dma, dma, dma((8,)), dma((8,)),
            dma((16,)), dma((16,)), dma((16,)), dma((16,)), dma((16,)), dma((16,)),
        ],
        compiler_params=pltpu.CompilerParams(collective_id=0, has_side_effects=True, vmem_limit_bytes=50 * 2**20),
        name="layer",
    )(*[pltpu.with_memory_space_constraint(a, pltpu.MemorySpace.HBM) for a in (
        tokens.reshape(512, 1024), context_positions.T, projection_weight, output_weight,
        norm_gain.reshape(1, -1), norm_bias.reshape(1, -1), projection_bias.reshape(1, -1),
        context_gain.reshape(1, -1), context_bias.reshape(1, -1), output_bias.reshape(1, -1))])
    return mixed.reshape(32, 16, 1024), context


def solution(mesh):
    return jax.shard_map(
        on_device,
        mesh=mesh,
        in_specs=(P("ns", "ew", None), P(), P(), P(), P(), P(), P(), P(), P(), P()),
        out_specs=(P("ns", "ew", None), P()),
        check_vma=False,
    )
```

time: 71.6 us -> 65.3 us (0.912)
  the two profiles are of different devices: /device:TPU:2 before, /device:TPU:24 now
where the time goes in v3:
time: 65.3 us
  Pallas kernels  62.8 us (96%)
  local copies, waits for them, and re-layouts  1.77 us (3%)
    pallas_call x1, Pallas kernels, on_device(): pl.pallas_call(layer, out_shape=(jax.ShapeDtypeStruct((512, 1024), BF16),...  62.8 us
    unnamed x2, local copies, waits for them, and re-layouts  1.77 us

profile of v3, /device:TPU:24, one launch (start us, length us, event | category | flops | bytes accessed | tf_op | source)
XLA Modules:
  0.0 65.3 jit_solution(8406754259694669587)
XLA Ops:
  0.6 62.8 %layer.1 = (bf16[512,1024]{1,0:T(8,128)(2,1)S(1)}, bf16[256,1024]{1,0:T(8,128)(2,1)S(1)}) custom-call(bf16[512,1024]{1,0:T(8,128)(2,1)} %bitcast.10, s32[64,256]{1,0:T(8,128)} %bitcast.11, bf16[1024,3072]{1,0:T(8,128)(2,1)} %w_hbm.1, bf16[1024,1024]{1,0:T(8,128)(2,1)} %wo_hbm.1, f32[1,1024]{1,0:T(1,128)} %bitcast.13, f32[1,1024]{1,0:T(1,128)} %bitcast.14, ...), custom_call_target="tpu_custom_call" | custom-call | tf_op jit(solution)/shard_map/layer/pallas_call | solution.py:387
  63.5 1.0 %copy.14 = bf16[32,16,1024]{2,1,0:T(8,128)(2,1)} copy(bf16[32,16,1024]{2,1,0:T(8,128)(2,1)S(1)} %bitcast.9) | data formatting | bytes 2097152
  64.5 0.8 %copy.15 = bf16[256,1024]{1,0:T(8,128)(2,1)} copy(bf16[256,1024]{1,0:T(8,128)(2,1)S(1)} %get-tuple-element.9) | data formatting | bytes 1048576

commit v4 on v2

--- a/solution.py
+++ b/solution.py
@@ -22,9 +22,9 @@
     return centre * lax.rsqrt(spread + 1e-05) * gain + bias
 
 
-def layer(tokens_hbm, pos_hbm, w_hbm, wo_hbm, gain, beta, wb, cgain, cbias, ob, out, ctx_out,
-          tokens, pos, wq, wk, wv, wo, normed, k, v, q2, att, near_o, near_m, near_l, near_bias,
-          s_a, s_b, p_a, p_b, ml_a, ml_b, cs, cp, cml, kc, vc, ctx,
+def layer(tokens_hbm, pos_hbm, w_hbm, wo_hbm, gain_hbm, beta_hbm, wb_hbm, cgain_hbm, cbias_hbm, ob_hbm, out, ctx_out,
+          gain, beta, wb, cgain, cbias, ob, tokens, pos, field, wq, wk, wv, wo, normed, k, v, q2, att, near_o, near_m, near_l, near_bias,
+          s_a, s_b, p_a, p_b, ml_a, ml_b, cs, cp, cml, cs2, cp2, cml2, kc, vc, ctx,
           rim, send_l, send_r, counts, partial, buf0, p1, buf1, p2, buf2, g,
           load, halo_s, halo_r, s0, r0, s1, r1, s2, r2, s3, r3, s4, r4):
     ns = lax.axis_index("ns")
@@ -41,8 +41,9 @@
 
     loads = [pltpu.make_async_copy(a, b, load.at[i]) for i, (a, b) in enumerate((
         (tokens_hbm, tokens), (pos_hbm, pos), (w_hbm.at[:, pl.ds(1024, 1024)], wk), (w_hbm.at[:, pl.ds(2048, 1024)], wv),
-        (w_hbm.at[:, pl.ds(0, 1024)], wq), (wo_hbm, wo)))]
-    for c in loads:
+        (w_hbm.at[:, pl.ds(0, 1024)], wq), (wo_hbm, wo), (gain_hbm, gain), (beta_hbm, beta), (wb_hbm, wb),
+        (cgain_hbm, cgain), (cbias_hbm, cbias), (ob_hbm, ob)))]
+    for c in loads[:2] + loads[6:] + loads[2:6]:
         c.start()
     loads[0].wait()
 
@@ -99,23 +100,24 @@
                 rim[t, at:at + 64, :] = jnp.zeros((64, 1024), BF16)
 
     loads[1].wait()
-
-    @pl.loop(0, 8)
+    lr = (pos[...] >> 8) - ns * 32
+    lc = (pos[...] & 255) - ew * 16
+    own = (lr >= 0) & (lr < 32) & (lc >= 0) & (lc < 16)
+    pos[...] = jnp.where(own, (lr & 7) * 16 + lc, -1)
+    field[...] = jnp.where(own, lax.shift_left(jnp.ones_like(lr), (lr >> 3) * 8), 0)
+
+    @pl.loop(0, 2)
     def _(t):
-        at = pos[...]
-        lr = (at >> 8) - ns * 32
-        lc = (at & 255) - ew * 16
-        own = (lr >= 0) & (lr < 32) & (lc >= 0) & (lc < 16)
-        own_id = jnp.where(own, lr * 16 + lc, -1)
         ids = lax.broadcasted_iota(jnp.int32, (64, 256), 0) + t * 64
-        total = jnp.zeros((64, 256), F32)
+        total = jnp.zeros((64, 256), jnp.int32)
         for p in range(64):
-            total = total + jnp.where(own_id[p:p + 1, :] == ids, 1.0, 0.0)
-        counts[rows_at(t * 64, 64), :] = total.astype(BF16)
-
-    @pl.loop(0, 4)
-    def _(t):
-        cols = rows_at(t * 256, 256)
+            total = total + jnp.where(pos[p:p + 1, :] == ids, field[p:p + 1, :], 0)
+        for i in range(4):
+            part = (total >> (8 * i)) & 255
+            counts[rows_at(i * 128 + t * 64, 64), :] = part.astype(F32).astype(BF16)
+
+    for t in range(2):
+        cols = slice(t * 512, t * 512 + 512)
         partial[:, cols] = lax.dot_general(counts[...], tokens[:, cols], TN, preferred_element_type=F32)
 
     pair = pltpu.make_async_remote_copy(
@@ -124,26 +126,26 @@
     pair.start()
 
     def project(weight, bias_at, dst, place):
-        @pl.loop(0, 4)
-        def _(n):
-            cols = rows_at(n * 256, 256)
-            y = jnp.dot(normed[...], weight[:, cols], preferred_element_type=F32)
-            y = (y + wb[:, rows_at(bias_at + n * 256, 256)]).astype(BF16)
-            for i in range(4):
-                dst[place[i]:place[i] + 128, cols] = y[i * 128:i * 128 + 128]
-
-    @pl.loop(0, 4)
-    def _(i):
-        rows = rows_at(i * 128, 128)
-        normed[rows, :] = norm_rows(tokens[rows, :].astype(F32), gain[...], beta[...]).astype(BF16)
+        size = 128 * len(place)
+        for n in range(2):
+            cols = slice(n * 512, n * 512 + 512)
+            y = jnp.dot(normed[0:size, :], weight[:, cols], preferred_element_type=F32)
+            y = (y + wb[:, bias_at + n * 512:bias_at + n * 512 + 512]).astype(BF16)
+            for i, at in enumerate(place):
+                dst[at:at + 128, cols] = y[i * 128:i * 128 + 128]
+
+    def norm_into(at, x):
+        normed[at:at + x.shape[0], :] = norm_rows(x.astype(F32), gain[...], beta[...]).astype(BF16)
+
+    for c in loads[6:]:
+        c.wait()
+    for i in range(2):
+        norm_into(i * 256, tokens[i * 256:i * 256 + 256, :])
 
     mid_own = (256, 512, 768, 1024)
     mid_side = (384, 640, 896, 1152)
     loads[2].wait()
     project(wk, 1024, k, mid_own)
-    loads[3].wait()
-    project(wv, 2048, v, mid_own)
-
     pair.wait()
 
     @pl.loop(0, 8)
@@ -156,19 +158,28 @@
                                             device_id=(to * 2 + core, ew), device_id_type=MESH)
     pl.loop(1, 8)(lambda d: stage1(d).start())
 
+    loads[3].wait()
+    project(wv, 2048, v, mid_own)
+
     low = lax.broadcasted_iota(jnp.int32, (128, 128), 1) < 64
     loads[4].wait()
 
-    @pl.loop(0, 4)
-    def _(n):
-        cols = rows_at(n * 256, 256)
+    for n in range(2):
+        cols = slice(n * 512, n * 512 + 512)
         y = jnp.dot(normed[...], wq[:, cols], preferred_element_type=F32)
         y = (y + wb[:, cols]).astype(BF16).astype(F32) * 0.125
         for b in range(4):
-            for i in range(2):
+            for i in range(4):
                 q = y[b * 128:b * 128 + 128, i * 128:i * 128 + 128]
-                q2[n * 2 + i, b * 256:b * 256 + 128, :] = jnp.where(low, q, 0.0).astype(BF16)
-                q2[n * 2 + i, b * 256 + 128:b * 256 + 256, :] = jnp.where(low, 0.0, q).astype(BF16)
+                q2[n * 4 + i, b * 256:b * 256 + 128, :] = jnp.where(low, q, 0.0).astype(BF16)
+                q2[n * 4 + i, b * 256 + 128:b * 256 + 256, :] = jnp.where(low, 0.0, q).astype(BF16)
+
+    pl.when(has_down)(go_up[0].wait_recv)
+    pl.when(has_up)(go_down[0].wait_recv)
+    norm_into(0, rim[0, 0:128, :])
+    norm_into(128, rim[5, 0:128, :])
+    project(wk, 1024, k, (0, 1280))
+    project(wv, 2048, v, (0, 1280))
 
     for i in range(2):
         pl.when(has_left)(go_right[i].wait_recv)
@@ -180,13 +191,6 @@
     pl.when(has_left)(go_right[2].wait_recv)
     pl.when(has_right)(go_left[2].wait_recv)
 
-    @pl.loop(0, 4)
-    def _(i):
-        normed[rows_at(i * 128, 128), :] = norm_rows(
-            rim[i + 1, 128:256, :].astype(F32), gain[...], beta[...]).astype(BF16)
-
-    project(wk, 1024, k, mid_side)
-
     pl.loop(1, 8)(lambda d: stage1(d).wait())
     total = p1[unit]
     for d in range(1, 8):
@@ -200,6 +204,9 @@
                                             device_id=(ns, to), device_id_type=MESH)
     pl.loop(1, 16)(lambda d: stage2(d).start())
 
+    for i in range(4):
+        norm_into(i * 128, rim[i + 1, 128:256, :])
+    project(wk, 1024, k, mid_side)
     project(wv, 2048, v, mid_side)
 
     def stage3(d):
@@ -287,35 +294,28 @@
                 near_m[qrows, lanes] = jnp.where(low, mlb[0, 0:128], mlb[0, 128:256])
                 near_l[qrows, lanes] = jnp.where(low, mlb[1, 0:128], mlb[1, 128:256])
 
+    pl.loop(1, 16)(lambda d: stage2(d).wait())
+    total = p2[ew]
+    for d in range(1, 16):
+        total = total + buf2[d]
+    g[ew] = total
+    pl.loop(1, 16)(lambda d: stage3(d).start())
+
     @pl.loop(0, 4)
     def _(t):
         @pl.when(t == 2)
         def _():
-            pl.when(has_down)(go_up[0].wait_recv)
-            pl.when(has_up)(go_down[0].wait_recv)
             when_all(has_left & has_down, [west_up.wait_recv])
             when_all(has_left & has_up, [west_down.wait_recv])
             when_all(has_right & has_down, [east_up.wait_recv])
             when_all(has_right & has_up, [east_down.wait_recv])
 
-            @pl.loop(0, 4)
-            def _(i):
-                normed[rows_at(i * 128, 128), :] = norm_rows(
-                    rim[i // 2 * 5, rows_at(lax.rem(i, 2) * 128, 128), :].astype(F32), gain[...], beta[...]).astype(BF16)
-            ends = (0, 128, 1280, 1408)
-            project(wk, 1024, k, ends)
-            project(wv, 2048, v, ends)
+            norm_into(0, rim[0, 128:256, :])
+            norm_into(128, rim[5, 128:256, :])
+            project(wk, 1024, k, (128, 1408))
+            project(wv, 2048, v, (128, 1408))
 
         band_step(t)
-
-        @pl.when(t == 0)
-        def _():
-            pl.loop(1, 16)(lambda d: stage2(d).wait())
-            total = p2[ew]
-            for d in range(1, 16):
-                total = total + buf2[d]
-            g[ew] = total
-            pl.loop(1, 16)(lambda d: stage3(d).start())
 
         @pl.when(t == 1)
         def _():
@@ -337,18 +337,12 @@
         for j in range(8):
             at = i * 128 + j * 16
             normed[at:at + 16, :] = ctx[i, j]
-    give = pltpu.make_async_copy(normed.at[pl.ds(0, 256)], ctx_out, load.at[0])
-    give.start()
-
-    for weight, bias_at, dst in ((wk, 1024, kc), (wv, 2048, vc)):
-        @pl.loop(0, 4)
-        def _(n):
-            cols = rows_at(n * 256, 256)
-            y = jnp.dot(normed[0:256, :], weight[:, cols], preferred_element_type=F32)
-            dst[:, cols] = (y + wb[:, rows_at(bias_at + n * 256, 256)]).astype(BF16)
-
-    @pl.loop(0, 8)
-    def _(p):
+    ctx_out[...] = normed[0:256, :]
+
+    project(wk, 1024, kc, (0, 128))
+    project(wv, 2048, vc, (0, 128))
+
+    def context_pair(p, cs, cp, cml):
         lanes = rows_at(p * 128, 128)
         for half in range(2):
             cs[half * 512:half * 512 + 512, :] = lax.dot_general(
@@ -368,15 +362,18 @@
             both = near_o[rows, lanes] * fn + oc * fc
             att[rows, lanes] = (both / (near_l[rows, lanes] * fn + lc * fc)).astype(BF16)
 
+    @pl.loop(0, 4)
+    def _(i):
+        context_pair(i * 2, cs, cp, cml)
+        context_pair(i * 2 + 1, cs2, cp2, cml2)
+
     loads[5].wait()
 
-    @pl.loop(0, 4)
-    def _(n):
-        cols = rows_at(n * 256, 256)
+    for n in range(2):
+        cols = slice(n * 512, n * 512 + 512)
         y = jnp.dot(att[...], wo[:, cols], preferred_element_type=F32)
         out[:, cols] = (tokens[:, cols].astype(F32) + y + ob[:, cols]).astype(BF16)
 
-    give.wait()
     when_all(has_left, [c.wait_send for c in go_left])
     when_all(has_right, [c.wait_send for c in go_right])
     when_all(has_up, [go_up[0].wait_send])
@@ -390,7 +387,7 @@
 def on_device(tokens, norm_gain, norm_bias, projection_weight, projection_bias, context_gain, context_bias,
               output_weight, output_bias, context_positions):
     vm = pl.BlockSpec(memory_space=pltpu.VMEM)
-    hbm = pl.BlockSpec(memory_space=pl.ANY)
+    hbm = pl.BlockSpec(memory_space=pltpu.MemorySpace.HBM)
     dma = pltpu.SemaphoreType.DMA
 
     def f32(*shape):
@@ -402,25 +399,27 @@
     mixed, context = pl.pallas_call(
         layer,
         out_shape=(jax.ShapeDtypeStruct((512, 1024), BF16), jax.ShapeDtypeStruct((256, 1024), BF16)),
-        in_specs=[hbm] * 4 + [vm] * 6,
-        out_specs=(vm, hbm),
+        in_specs=[hbm] * 10,
+        out_specs=(vm, vm),
         scratch_shapes=[
-            b16(512, 1024), pltpu.VMEM((64, 256), jnp.int32), b16(1024, 1024), b16(1024, 1024), b16(1024, 1024),
+            f32(1, 1024), f32(1, 1024), f32(1, 3072), f32(1, 1024), f32(1, 1024), f32(1, 1024),
+            b16(512, 1024), pltpu.VMEM((64, 256), jnp.int32), pltpu.VMEM((64, 256), jnp.int32), b16(1024, 1024), b16(1024, 1024), b16(1024, 1024),
             b16(1024, 1024), b16(512, 1024), b16(1536, 1024), b16(1536, 1024), b16(8, 1024, 128), b16(512, 1024),
             f32(512, 1024), f32(512, 1024), f32(512, 1024), f32(128, 768),
             f32(256, 768), f32(256, 768), b16(256, 768), b16(256, 768), f32(2, 256, 128), f32(2, 256, 128),
-            f32(1024, 256), b16(1024, 256), f32(2, 1024, 128), b16(256, 1024), b16(256, 1024), b16(2, 8, 16, 1024),
+            f32(1024, 256), b16(1024, 256), f32(2, 1024, 128), f32(1024, 256), b16(1024, 256), f32(2, 1024, 128), b16(256, 1024), b16(256, 1024), b16(2, 8, 16, 1024),
             b16(6, 256, 1024), b16(4, 64, 1024), b16(4, 64, 1024),
             b16(512, 256), f32(256, 1024), f32(128, 1024), f32(8, 16, 1024), f32(8, 16, 1024),
             f32(16, 8, 128), f32(16, 8, 128), f32(16, 8, 128),
-            dma((6,)), dma((12,)), dma((12,)), dma, dma, dma((8,)), dma((8,)),
+            dma((12,)), dma((12,)), dma((12,)), dma, dma, dma((8,)), dma((8,)),
             dma((16,)), dma((16,)), dma((16,)), dma((16,)), dma((16,)), dma((16,)),
         ],
-        compiler_params=pltpu.CompilerParams(collective_id=0, has_side_effects=True, vmem_limit_bytes=60 * 2**20),
+        compiler_params=pltpu.CompilerParams(collective_id=0, has_side_effects=True, vmem_limit_bytes=54 * 2**20),
         name="layer",
-    )(tokens.reshape(512, 1024), context_positions.T, projection_weight, output_weight,
-      norm_gain.reshape(1, -1), norm_bias.reshape(1, -1), projection_bias.reshape(1, -1),
-      context_gain.reshape(1, -1), context_bias.reshape(1, -1), output_bias.reshape(1, -1))
+    )(*[pltpu.with_memory_space_constraint(a, pltpu.MemorySpace.HBM) for a in (
+        tokens.reshape(512, 1024), context_positions.T, projection_weight, output_weight,
+        norm_gain.reshape(1, -1), norm_bias.reshape(1, -1), projection_bias.reshape(1, -1),
+        context_gain.reshape(1, -1), context_bias.reshape(1, -1), output_bias.reshape(1, -1))])
     return mixed.reshape(32, 16, 1024), context
 
 

time: 71.6 us -> 66.9 us (0.934); the launches traced: 70.4 us -> 66.7 us
  Pallas kernels: 65.6 us -> 61.9 us
    pallas_call x1, Pallas kernels: 65.6 us -> 61.9 us  [on_device(): pl.pallas_call(layer, out_shape=(jax.ShapeDtypeStruct((512, 1024), BF16),...]
where the time goes in v4:
time: 66.9 us; the launch traced here: 66.7 us
  Pallas kernels  61.9 us (93%)
  local copies, waits for them, and re-layouts  4.17 us (6%)
    pallas_call x1, Pallas kernels, on_device(): pl.pallas_call(layer, out_shape=(jax.ShapeDtypeStruct((512, 1024), BF16),...  61.9 us
    unnamed x2, local copies, waits for them, and re-layouts  4.17 us

profile of v4, /device:TPU:2, one launch (start us, length us, event | category | flops | bytes accessed | tf_op | source)
XLA Modules:
  0.0 66.7 jit_solution(14071899699300642537)
XLA Ops:
  0.6 61.9 %layer.1 = (bf16[512,1024]{1,0:T(8,128)(2,1)}, bf16[256,1024]{1,0:T(8,128)(2,1)}) custom-call(bf16[512,1024]{1,0:T(8,128)(2,1)} %bitcast.9, s32[64,256]{1,0:T(8,128)} %bitcast.11, bf16[1024,3072]{1,0:T(8,128)(2,1)} %w_hbm.1, bf16[1024,1024]{1,0:T(8,128)(2,1)} %wo_hbm.1, f32[1,1024]{1,0:T(1,128)} %bitcast.13, f32[1,1024]{1,0:T(1,128)} %bitcast.14, ...), custom_call_target="tpu_custom_call" | custom-call | tf_op jit(solution)/shard_map/layer/pallas_call | solution.py:399
  62.6 2.3 %copy.14 = bf16[32,16,1024]{2,1,0:T(8,128)(2,1)} copy(bf16[32,16,1024]{2,1,0:T(8,128)(2,1)} %bitcast.10) | data formatting | bytes 2097152
  64.9 1.9 %copy.15 = bf16[256,1024]{1,0:T(8,128)(2,1)} copy(bf16[256,1024]{1,0:T(8,128)(2,1)} %get-tuple-element.9) | data formatting | bytes 1048576

commit v5 on v4

--- a/solution.py
+++ b/solution.py
@@ -414,7 +414,7 @@
             dma((12,)), dma((12,)), dma((12,)), dma, dma, dma((8,)), dma((8,)),
             dma((16,)), dma((16,)), dma((16,)), dma((16,)), dma((16,)), dma((16,)),
         ],
-        compiler_params=pltpu.CompilerParams(collective_id=0, has_side_effects=True, vmem_limit_bytes=54 * 2**20),
+        compiler_params=pltpu.CompilerParams(collective_id=0, has_side_effects=True, vmem_limit_bytes=50 * 2**20),
         name="layer",
     )(*[pltpu.with_memory_space_constraint(a, pltpu.MemorySpace.HBM) for a in (
         tokens.reshape(512, 1024), context_positions.T, projection_weight, output_weight,

time: 66.9 us -> 63.2 us (0.945)
  local copies, waits for them, and re-layouts: 4.17 us -> 1.77 us
  Pallas kernels: 61.9 us -> 60.7 us
    unnamed x2, local copies, waits for them, and re-layouts: 4.17 us -> 1.77 us
    pallas_call x1, Pallas kernels: 61.9 us -> 60.7 us  [on_device(): pl.pallas_call(layer, out_shape=(jax.ShapeDtypeStruct((512, 1024), BF16),...]
where the time goes in v5:
time: 63.2 us
  Pallas kernels  60.7 us (96%)
  local copies, waits for them, and re-layouts  1.77 us (3%)
  between operations  0.64 us (1%)
    pallas_call x1, Pallas kernels, on_device(): pl.pallas_call(layer, out_shape=(jax.ShapeDtypeStruct((512, 1024), BF16),...  60.7 us
    unnamed x2, local copies, waits for them, and re-layouts  1.77 us

profile of v5, /device:TPU:2, one launch (start us, length us, event | category | flops | bytes accessed | tf_op | source)
XLA Modules:
  0.0 63.2 jit_solution(2577735326693453478)
XLA Ops:
  0.6 60.7 %layer.1 = (bf16[512,1024]{1,0:T(8,128)(2,1)S(1)}, bf16[256,1024]{1,0:T(8,128)(2,1)S(1)}) custom-call(bf16[512,1024]{1,0:T(8,128)(2,1)} %bitcast.10, s32[64,256]{1,0:T(8,128)} %bitcast.11, bf16[1024,3072]{1,0:T(8,128)(2,1)} %w_hbm.1, bf16[1024,1024]{1,0:T(8,128)(2,1)} %wo_hbm.1, f32[1,1024]{1,0:T(1,128)} %bitcast.13, f32[1,1024]{1,0:T(1,128)} %bitcast.14, ...), custom_call_target="tpu_custom_call" | custom-call | tf_op jit(solution)/shard_map/layer/pallas_call | solution.py:399
  61.4 1.0 %copy.14 = bf16[32,16,1024]{2,1,0:T(8,128)(2,1)} copy(bf16[32,16,1024]{2,1,0:T(8,128)(2,1)S(1)} %bitcast.9) | data formatting | bytes 2097152
  62.4 0.8 %copy.15 = bf16[256,1024]{1,0:T(8,128)(2,1)} copy(bf16[256,1024]{1,0:T(8,128)(2,1)S(1)} %get-tuple-element.9) | data formatting | bytes 1048576

commit v6 on v5

--- a/solution.py
+++ b/solution.py
@@ -78,11 +78,11 @@
                 c()
 
     pl.semaphore_wait(barrier, 30)
+    pl.when(has_up)(go_up[0].start)
+    pl.when(has_down)(go_down[0].start)
     for i in range(3):
         pl.when(has_left)(go_left[i].start)
         pl.when(has_right)(go_right[i].start)
-    pl.when(has_up)(go_up[0].start)
-    pl.when(has_down)(go_down[0].start)
 
     @pl.when(jnp.logical_not(has_up))
     def _():

time: 63.2 us -> 63.2 us (level)
  no operation moved by 1% of the time
where the time goes in v6:
time: 63.2 us
  Pallas kernels  60.7 us (96%)
  local copies, waits for them, and re-layouts  1.77 us (3%)
  between operations  0.64 us (1%)
    pallas_call x1, Pallas kernels, on_device(): pl.pallas_call(layer, out_shape=(jax.ShapeDtypeStruct((512, 1024), BF16),...  60.7 us
    unnamed x2, local copies, waits for them, and re-layouts  1.77 us

profile of v6, /device:TPU:2, one launch (start us, length us, event | category | flops | bytes accessed | tf_op | source)
XLA Modules:
  0.0 63.2 jit_solution(12585779020467691258)
XLA Ops:
  0.6 60.7 %layer.1 = (bf16[512,1024]{1,0:T(8,128)(2,1)S(1)}, bf16[256,1024]{1,0:T(8,128)(2,1)S(1)}) custom-call(bf16[512,1024]{1,0:T(8,128)(2,1)} %bitcast.10, s32[64,256]{1,0:T(8,128)} %bitcast.11, bf16[1024,3072]{1,0:T(8,128)(2,1)} %w_hbm.1, bf16[1024,1024]{1,0:T(8,128)(2,1)} %wo_hbm.1, f32[1,1024]{1,0:T(1,128)} %bitcast.13, f32[1,1024]{1,0:T(1,128)} %bitcast.14, ...), custom_call_target="tpu_custom_call" | custom-call | tf_op jit(solution)/shard_map/layer/pallas_call | solution.py:399
  61.4 1.0 %copy.14 = bf16[32,16,1024]{2,1,0:T(8,128)(2,1)} copy(bf16[32,16,1024]{2,1,0:T(8,128)(2,1)S(1)} %bitcast.9) | data formatting | bytes 2097152
  62.4 0.8 %copy.15 = bf16[256,1024]{1,0:T(8,128)(2,1)} copy(bf16[256,1024]{1,0:T(8,128)(2,1)S(1)} %get-tuple-element.9) | data formatting | bytes 1048576
